TPU v7x, 32 devices: a whole 2x2x4 slice. The times are simulated.
32 devices in a mesh: run: 1, row: 16 (over z, y, core), col: 1, seg: 2 (over x).
Axes of the slice: x: 2, y: 2, z: 4, core: 2. Of those that a mesh axis runs over, the one named last changes fastest.
Arguments:
- traces: bfloat16 [2, 1024, 2048], P(('run', 'seg'), 'row', 'col'), may hold values from -30 to 30
- live_mask: int32 [1024], P(('run', 'row')), may hold values 0 or 1
- sources: int32 [64], replicated, may hold values from 0 to 1023
- owners: int32 [64, 1], replicated, may hold values from 0 to 15; in each aligned block of 64 rows (0 to 63, 64 to 127, ...) at most 12 rows name the same one
Outputs:
- gathers: bfloat16 [192, 16, 64, 256], P(('run', 'row'), None, ('col', 'seg'))
Inputs may be any that keep to these rules, and one draw needn't show every extreme that they name: `owners`: at most 12 sources share an owner, and some owner has exactly 12.
All inputs are finite; a program needn't handle non-finite values. No bound on the sum of `live_mask` on one device may be relied on, other than what follows from the above.
Results may differ from a plain program's by a relative error of at most 0.024.
Values may be sent and summed in bfloat16 or wider, within the bound.
A program may use at most 64 MiB of HBM per device.

v0:
```python
import math

import jax
import jax.numpy as jnp
from jax import lax
from jax.sharding import PartitionSpec as P

NT = 2048
NF = 1024
LAGS = 256
BAND = 64


two_pi = 2.0 * math.pi


def turn_table(first_ids, second_ids, period):
    product = first_ids[:, None] * second_ids[None, :] % period
    return product.astype(jnp.float32) * (two_pi / period)


def lag_matrix(bin_ids):
    lag_ids = jnp.arange(LAGS, dtype=jnp.int32) - LAGS // 2 + NT
    lag_angles = turn_table(bin_ids, lag_ids, NT)
    return jnp.concatenate(
        [jnp.cos(lag_angles).astype(jnp.bfloat16), -jnp.sin(lag_angles).astype(jnp.bfloat16)],
        axis=0,
    )


def correlate(recv_real, recv_imag, real_source, imag_source, lag_table):
    cross_real = (
        real_source[:, None, :] * recv_real[:, :, None]
        + imag_source[:, None, :] * recv_imag[:, :, None]
    ).astype(jnp.bfloat16)
    cross_imag = (
        imag_source[:, None, :] * recv_real[:, :, None]
        - real_source[:, None, :] * recv_imag[:, :, None]
    ).astype(jnp.bfloat16)
    stacked_cross = jnp.concatenate([cross_real, cross_imag], axis=0)
    return jnp.einsum("fl,fgv->gvl", lag_table, stacked_cross, preferred_element_type=jnp.float32)


def local(traces, live_mask, sources, owners):
    col_count = lax.axis_size("col")
    seg_count = lax.axis_size("seg")
    row_count = lax.axis_size("row")
    samples = traces[0]
    channels = samples.shape[0]
    local_width = samples.shape[1]
    num_sources = sources.shape[0]
    first_sample = lax.axis_index("col") * local_width
    half_bins = NF // col_count
    sample_ids = first_sample + jnp.arange(local_width, dtype=jnp.int32)
    bin_ids = jnp.arange(half_bins * lax.axis_size("col"), dtype=jnp.int32)
    angles = turn_table(sample_ids, bin_ids, NT)
    cosine = jnp.cos(angles).astype(jnp.bfloat16)
    sine_table = jnp.sin(angles).astype(jnp.bfloat16)
    real_part = jnp.einsum("tf,ct->fc", cosine, samples, preferred_element_type=jnp.float32)
    imag_part = -jnp.einsum("tf,ct->fc", sine_table, samples, preferred_element_type=jnp.float32)
    spectra = lax.psum_scatter(
        jnp.concatenate([real_part, imag_part], axis=1).astype(jnp.bfloat16),
        "col",
        scatter_dimension=0,
        tiled=True,
    ).astype(jnp.float32)
    squares = (spectra * spectra).reshape(half_bins // BAND, BAND, 2, channels)
    band_power = jnp.sum(squares, axis=(1, 2)) / (2 * BAND) + 1e-05
    scaling = live_mask.astype(jnp.float32)[None, :] / jnp.sqrt(band_power)
    scaling = jnp.repeat(scaling, BAND, axis=0)
    whitened = (
        (spectra.reshape(half_bins, 2, channels) * scaling[:, None, :])
        .reshape(half_bins, 2 * channels)
        .astype(jnp.bfloat16)
    )
    white_real = whitened[:, :channels]
    white_imag = whitened[:, channels:]
    everyone = lax.all_gather(whitened, "row", axis=1, tiled=True)
    block_ids = sources // channels
    within = sources % channels
    real_cols = block_ids * (2 * channels) + within
    source_real = jnp.take(everyone, real_cols, axis=1)
    source_imag = jnp.take(everyone, real_cols + channels, axis=1)
    receivers = channels // (col_count * seg_count)
    bin_ids = lax.axis_index("col") * half_bins + jnp.arange(half_bins, dtype=jnp.int32)
    lag_table = lag_matrix(bin_ids)
    real_source = source_real.astype(jnp.float32)
    imag_source = source_imag.astype(jnp.float32)

    def one_group(offset):
        recv_real = lax.dynamic_slice_in_dim(white_real, offset, receivers, 1).astype(jnp.float32)
        recv_imag = lax.dynamic_slice_in_dim(white_imag, offset, receivers, 1).astype(jnp.float32)
        return correlate(recv_real, recv_imag, real_source, imag_source, lag_table)

    offsets = (
        jnp.arange(receivers * lax.axis_size(("col", "seg")) // receivers, dtype=jnp.int32)
        * receivers
    )
    blocks = lax.map(one_group, offsets)
    stacked = lax.psum_scatter(
        blocks.reshape(receivers * lax.axis_size(("col", "seg")), num_sources, LAGS).astype(
            jnp.bfloat16
        ),
        ("col", "seg"),
        scatter_dimension=0,
        tiled=True,
    ).astype(jnp.float32)
    mean_sq = jnp.mean(stacked * stacked, axis=-1, keepdims=True)
    normed = (stacked / jnp.sqrt(mean_sq + 1e-06)).astype(jnp.bfloat16)
    capacity = 3 * num_sources // row_count
    owner_ids = owners[:, 0]
    order_ids = jnp.arange(num_sources, dtype=jnp.int32)
    earlier = (owner_ids[:, None] == owner_ids[None, :]) & (order_ids[None, :] < order_ids[:, None])
    slot_rank = jnp.sum(earlier.astype(jnp.int32), axis=1)
    slot_ids = owner_ids * capacity + slot_rank
    placing = (
        jnp.arange(row_count * capacity, dtype=jnp.int32)[:, None] == slot_ids[None, :]
    ).astype(jnp.bfloat16)
    outgoing = jnp.einsum(
        "sv,gvl->sgl", placing, normed, preferred_element_type=jnp.float32
    ).astype(jnp.bfloat16)
    return lax.all_to_all(outgoing[:, None], "row", split_axis=0, concat_axis=1, tiled=True)


def solution(mesh):
    placed = (P(("run", "seg"), "row", "col"), P(("run", "row")), P(), P())
    return jax.shard_map(
        local,
        mesh=mesh,
        in_specs=placed,
        out_specs=P(("run", "row"), None, ("col", "seg"), None),
        check_vma=False,
    )
```

profile of v0, /device:TPU:0, one launch (start us, length us, event | category | flops | bytes accessed | tf_op | source)
XLA Modules:
  0.0 270.7 jit_solution(1408020758581116476)
XLA Ops:
  6.5 0.0 copy-start
  6.5 0.0 all-gather.2.cloned.1.call-start
  6.5 0.9 copy-done
  7.5 31.3 %fusion.21 = bf16[1024,64]{0,1:T(8,128)(2,1)S(1)} fusion(bf16[1,64,2048]{2,1,0:T(8,128)(2,1)S(1)} %copy-done), kind=kOutput, calls=%fused_computation.35 | convolution fusion | flops 300023808 | bytes 393216 | tf_op jit(solution)/shard_map/tf,ct->fc/dot_general | solution.py:60
  38.8 0.0 copy-start.4
  38.8 31.2 %fusion.22 = bf16[1024,64]{0,1:T(8,128)(2,1)S(1)} fusion(bf16[1,64,2048]{2,1,0:T(8,128)(2,1)S(1)} %copy-done), kind=kOutput, calls=%fused_computation.36 | convolution fusion | flops 299958272 | bytes 393216 | tf_op jit(solution)/shard_map/tf,ct->fc/dot_general | solution.py:59
  70.1 0.0 copy-start.3
  70.1 0.3 mul.149
  70.4 0.2 reduce_sum.28
  70.6 0.1 copy.15
  70.7 0.0 copy-done.4
  70.7 0.1 copy.16
  70.8 0.2 broadcast_in_dim.19
  71.0 0.2 mul.150
  71.2 0.8 multiply_convert_fusion
  72.0 0.0 all-gather.2.cloned.1.call-update
  72.0 0.0 reduce-scatter.2.cloned.1.call-start
  72.1 0.0 copy-done.3
  72.2 1.0 fusion.48
  73.1 4.2 %cosine_convert_fusion.4 = bf16[1024,256]{1,0:T(8,128)(2,1)S(1)} fusion(s32[256]{0:T(256)S(1)} %iota_add_fusion), kind=kLoop, calls=%fused_computation.43 | loop fusion | flops 3932160 | bytes 525312 | tf_op jit(solution)/shard_map/convert_element_type | solution.py:26
  77.3 4.0 %fusion.31 = bf16[1024,256]{1,0:T(8,128)(2,1)S(1)} fusion(s32[256]{0:T(256)S(1)} %iota_add_fusion), kind=kLoop, calls=%fused_computation.47 | loop fusion | flops 4718592 | bytes 525312 | tf_op jit(solution)/shard_map/neg | solution.py:26
  81.4 1.0 pad_maximum_fusion
  82.4 43.1 %all-gather.2.cloned.1.call-done = bf16[1024,2048]{0,1:T(8,128)(2,1)} async-done(((bf16[1024,128]{0,1:T(8,128)(2,1)}), bf16[1024,2048]{0,1:T(8,128)(2,1)}) %all-gather.2.cloned.1.call-update) | async-done | bytes 4194320 | tf_op jit(solution)/shard_map/all_gather | solution.py:78
  125.5 3.5 %gather_fusion = bf16[64,1024]{1,0:T(8,128)(2,1)S(1)} fusion(bf16[1024,2048]{0,1:T(8,128)(2,1)} %all-gather.2.cloned.1.call-done, s32[1024]{0:T(1024)S(1)} %pad_clamp_fusion.1), kind=kCustom, calls=%fused_computation.clone | custom fusion | bytes 262400 | tf_op jit(solution)/shard_map/jit(_take)/gather | solution.py:82
  129.0 3.5 %gather_fusion.1 = bf16[64,1024]{1,0:T(8,128)(2,1)S(1)} fusion(bf16[1024,2048]{0,1:T(8,128)(2,1)} %all-gather.2.cloned.1.call-done, s32[1024]{0:T(1024)S(1)} %pad_clamp_fusion), kind=kCustom, calls=%fused_computation.1.clone | custom fusion | bytes 262400 | tf_op jit(solution)/shard_map/jit(_take)/gather | solution.py:83
  132.6 0.1 bitcast_convert_fusion
  132.7 0.0 copy-start.5
  132.7 16.3 %while.10 = (s32[]{:T(128)}, bf16[2,32,64,256]{3,2,1,0:T(8,128)(2,1)S(1)}, f32[1024,64]{0,1:T(8,128)S(1)}, s32[2]{0:T(128)S(1)}, bf16[1024,64]{0,1:T(8,128)(2,1)...) while((s32[]{:T(128)}, ...), condition=%wide.region_3.5_spmd, body=%wide.region_2.4_spmd.sunk | while | flops 2181103616 | bytes 25297088 | solution.py:99
  132.7 0.7 dynamic_slice.15
  135.5 0.0 copy-start.2
  135.5 2.8 %add_convert_fusion.2 = (bf16[1024,32,64]{0,2,1:T(8,128)(2,1)S(1)}, bf16[1024,32,64]{0,2,1:T(8,128)(2,1)S(1)}) fusion(f32[1024,32]{0,1:T(8,128)S(1)} %get-tuple-element.129, f32[1024,64]{0,1:T(8,128)S(1)} %get-tuple-element.160, f32[1024,32]{0,1:T(8,128)S(1)} %get-tuple-element.130, f32[1024,64]{0,1:T(8,128)S(1)} %get-tuple-element.157), kind=kLoop, calls=%fused_computation.7.clone.1 | loop fusion | flops 16777216 | bytes 9175040 | tf_op jit(solution)/shard_map/while/body/eval_jaxpr/convert_element_type | solution.py:35
  138.3 0.0 copy-done.2
  138.3 2.5 bitcast_dynamic-update-slice_fusion.2
  140.9 0.7 dynamic_slice.15
  143.7 0.0 copy-start.2
  143.7 2.8 %add_convert_fusion.2 = (bf16[1024,32,64]{0,2,1:T(8,128)(2,1)S(1)}, bf16[1024,32,64]{0,2,1:T(8,128)(2,1)S(1)}) fusion(f32[1024,32]{0,1:T(8,128)S(1)} %get-tuple-element.129, f32[1024,64]{0,1:T(8,128)S(1)} %get-tuple-element.160, f32[1024,32]{0,1:T(8,128)S(1)} %get-tuple-element.130, f32[1024,64]{0,1:T(8,128)S(1)} %get-tuple-element.157), kind=kLoop, calls=%fused_computation.7.clone.1 | loop fusion | flops 16777216 | bytes 9175040 | tf_op jit(solution)/shard_map/while/body/eval_jaxpr/convert_element_type | solution.py:35
  146.5 0.0 copy-done.2
  146.5 2.5 bitcast_dynamic-update-slice_fusion.2
  149.0 0.0 copy-start.1
  149.1 1.3 copy-done.1
  150.4 0.0 reduce-scatter.2.cloned.1.call-update
  150.4 0.2 convert_reduce_fusion
  150.6 30.3 %reduce-scatter.2.cloned.1.call-done = bf16[32,64,256]{2,1,0:T(8,128)(2,1)} async-done(((bf16[64,64,256]{2,1,0:T(8,128)(2,1)}), bf16[32,64,256]{2,1,0:T(8,128)(2,1)}) %reduce-scatter.2.cloned.1.call-update) | async-done | bytes 1048592 | tf_op jit(solution)/shard_map/reduce_scatter | solution.py:100
  180.9 1.6 fusion.18
  182.4 2.3 convert_bitcast_fusion
  184.8 1.8 copy.17
  186.6 75.2 %all_to_all.18 = bf16[192,1,32,256]{3,2,1,0:T(8,128)(2,1)S(1)} all-to-all(bf16[192,1,32,256]{3,2,1,0:T(8,128)(2,1)S(1)} %copy.17), channel_id=1, replica_groups=mesh['run'=1,'row'=16,'col'=1,'seg'=2] {'row'}, dimensions={0} | all-to-all | bytes 6291456 | tf_op jit(solution)/shard_map/all_to_all | solution.py:122
  261.8 2.1 copy.18
  (16 shorter events, 0.2 us)
Async XLA Ops:
  6.5 1.0 copy-start
  6.5 119.0 %all-gather.2.cloned.1.call-start = ((), (), s32[]{:S(2)}) async-start(), calls=%async_computation.2 | async-start | bytes 4456448 | tf_op jit(solution)/shard_map/all_gather | solution.py:78
  38.8 31.9 %copy-start.4 = (s32[64]{0:T(128)S(1)}, s32[64]{0:T(128)}, u32[]{:S(2)}) copy-start(s32[64]{0:T(128)} %param.9) | copy-start | bytes 772
  70.1 2.0 copy-start.3
  72.0 108.9 %reduce-scatter.2.cloned.1.call-start = ((), (), s32[]{:S(2)}) async-start(), calls=%async_computation.3 | async-start | bytes 3145728 | tf_op jit(solution)/shard_map/reduce_scatter | solution.py:100
  132.7 17.7 %copy-start.5 = (s32[64,1]{0,1:T(1,128)S(1)}, s32[64,1]{0,1:T(1,128)}, u32[]{:S(2)}) copy-start(s32[64,1]{0,1:T(1,128)} %param.11) | copy-start | bytes 772
  135.5 2.8 %copy-start.2 = (bf16[2048,256]{1,0:T(8,128)(2,1)S(1)}, bf16[2048,256]{1,0:T(8,128)(2,1)}, u32[]{:S(2)}) copy-start(bf16[2048,256]{1,0:T(8,128)(2,1)} %get-tuple-element.162) | copy-start | bytes 3145732 | tf_op jit(solution)/shard_map/while
  143.7 2.8 %copy-start.2 = (bf16[2048,256]{1,0:T(8,128)(2,1)S(1)}, bf16[2048,256]{1,0:T(8,128)(2,1)}, u32[]{:S(2)}) copy-start(bf16[2048,256]{1,0:T(8,128)(2,1)} %get-tuple-element.162) | copy-start | bytes 3145732 | tf_op jit(solution)/shard_map/while
  149.0 1.3 copy-start.1
Sparse Core Ops, SparseCore 0:
  72.1 53.3 all-gather.1
  150.5 30.2 reduce-scatter.1
where the time goes:
time: 271 us
  blocking collectives  75.2 us (28%)
  waiting for transfers between devices  73.4 us (27%)
  matrix products  70 us (26%)
  other arithmetic  17.9 us (7%)
  local copies, waits for them, and re-layouts  16.3 us (6%)
  between operations  13.6 us (5%)
  loops' own time  4.26 us (2%)
    all_to_all x1, blocking collectives, local(): lax.all_to_all(outgoing[:, None], 'row', split_axis=0, concat_axis=1, til...  75.2 us
    all_gather x1, waiting for transfers between devices, local(): everyone = lax.all_gather(whitened, 'row', axis=1, tiled=True)  43.1 us
    dot_general x1, matrix products, local(): jnp.einsum('tf,ct->fc', sine_table, samples, preferred_element_type=jnp.f...  31.3 us
    dot_general x1, matrix products, local(): jnp.einsum('tf,ct->fc', cosine, samples, preferred_element_type=jnp.float32)  31.2 us
    reduce_scatter x1, waiting for transfers between devices, local(): lax.psum_scatter(blocks.reshape(receivers * lax.axis_size(('col', 'seg'))...  30.3 us
    convert_element_type x2, other arithmetic, correlate(): cross_real = (real_source[:, None, :] * recv_real[:, :, None] + imag_sour...  5.58 us
  transfers between devices with their start and end apart: 2, of which 2 were waited for; matrix products, arithmetic and copies ran while one was open for 4% of the time, Pallas kernels for 0%

commit v1 on v0

--- a/solution.py
+++ b/solution.py
@@ -1,8 +1,12 @@
 import math
+from functools import partial
 
 import jax
 import jax.numpy as jnp
+import numpy as np
 from jax import lax
+from jax.experimental import pallas as pl
+from jax.experimental.pallas import tpu as pltpu
 from jax.sharding import PartitionSpec as P
 
 NT = 2048
@@ -122,10 +126,116 @@
     return lax.all_to_all(outgoing[:, None], "row", split_axis=0, concat_axis=1, tiled=True)
 
 
+def host_tables(num_samples):
+    samples = np.arange(num_samples, dtype=np.int64)
+    bins = np.arange(NF, dtype=np.int64)
+    angles = (samples[:, None] * bins[None, :] % NT) * (two_pi / NT)
+    forward = np.concatenate([np.cos(angles), -np.sin(angles)], axis=1)
+    lags = np.arange(LAGS, dtype=np.int64) - LAGS // 2 + NT
+    lag_angles = (bins[:, None] * lags[None, :] % NT) * (two_pi / NT)
+    back = np.concatenate([np.cos(lag_angles), -np.sin(lag_angles)], axis=0)
+    return forward.astype(jnp.bfloat16), back.astype(jnp.bfloat16)
+
+
+def whitened_spectra(samples, forward):
+    rows = samples.shape[0]
+    spectra = jnp.dot(samples, forward, preferred_element_type=jnp.float32)
+    power = jnp.sum((spectra * spectra).reshape(rows, 2, NF // BAND, BAND), axis=(1, 3))
+    scaling = 1.0 / jnp.sqrt(power / (2 * BAND) + 1e-05)
+    scaling = jnp.repeat(scaling, BAND, axis=1)
+    return (spectra * jnp.concatenate([scaling, scaling], axis=1)).astype(jnp.bfloat16)
+
+
+def gather_kernel(recv_ref, source_ref, back_ref, out_ref, cross_ref):
+    segments, slots, _ = source_ref.shape
+    receivers = recv_ref.shape[2]
+    for slot in range(slots):
+        real = imag = None
+        for seg in range(segments):
+            recv_real = recv_ref[0, seg, :, :NF]
+            recv_imag = recv_ref[0, seg, :, NF:]
+            source_real = source_ref[seg, slot : slot + 1, :NF]
+            source_imag = source_ref[seg, slot : slot + 1, NF:]
+            term_real = source_real * recv_real + source_imag * recv_imag
+            term_imag = source_imag * recv_real - source_real * recv_imag
+            real = term_real if real is None else real + term_real
+            imag = term_imag if imag is None else imag + term_imag
+        rows = pl.ds(slot * receivers, receivers)
+        cross_ref[rows, :NF] = real
+        cross_ref[rows, NF:] = imag
+    stacked = jnp.dot(cross_ref[...], back_ref[...], preferred_element_type=jnp.float32)
+    mean_sq = jnp.mean(stacked * stacked, axis=-1, keepdims=True)
+    normed = stacked * lax.rsqrt(mean_sq + 1e-06)
+    out_ref[...] = normed.astype(out_ref.dtype).reshape(out_ref.shape)
+
+
+def correlate_gathers(everyone, sources, back):
+    blocks, segments, receivers, width = everyone.shape
+    slots = sources.shape[1]
+    return pl.pallas_call(
+        gather_kernel,
+        grid=(blocks,),
+        in_specs=[
+            pl.BlockSpec((1, segments, receivers, width), lambda b: (b, 0, 0, 0)),
+            pl.BlockSpec((segments, slots, width), lambda b: (0, 0, 0)),
+            pl.BlockSpec((width, LAGS), lambda b: (0, 0)),
+        ],
+        out_specs=pl.BlockSpec((slots, 1, receivers, LAGS), lambda b: (0, b, 0, 0)),
+        out_shape=jax.ShapeDtypeStruct((slots, blocks, receivers, LAGS), jnp.bfloat16),
+        scratch_shapes=[pltpu.VMEM((slots * receivers, width), jnp.bfloat16)],
+        compiler_params=pltpu.CompilerParams(vmem_limit_bytes=40 << 20),
+        cost_estimate=pl.CostEstimate(
+            flops=2 * slots * blocks * receivers * width * LAGS,
+            bytes_accessed=2 * blocks * receivers * (segments * width + slots * LAGS),
+            transcendentals=0,
+        ),
+    )(everyone, sources, back)
+
+
+def slot_channels(sources, owners, row_count):
+    num_sources = sources.shape[0]
+    capacity = 3 * num_sources // row_count
+    owner_ids = owners[:, 0]
+    order_ids = jnp.arange(num_sources, dtype=jnp.int32)
+    earlier = (owner_ids[:, None] == owner_ids[None, :]) & (order_ids[None, :] < order_ids[:, None])
+    slot_ids = owner_ids * capacity + jnp.sum(earlier.astype(jnp.int32), axis=1)
+    placing = jnp.arange(row_count * capacity, dtype=jnp.int32)[:, None] == slot_ids[None, :]
+    return jnp.sum(jnp.where(placing, sources[None, :] + 1, 0), axis=1) - 1
+
+
+def paired(forward, back, traces, live_mask, sources, owners):
+    row_count = lax.axis_size("row")
+    seg = lax.axis_index("seg")
+    channels, width = traces.shape[1:]
+    receivers = channels // 2
+    samples = traces[0] * live_mask.astype(traces.dtype)[:, None]
+    channel_of = slot_channels(sources, owners, row_count)
+    first = lax.axis_index("row") * channels
+    picking = channel_of[:, None] == first + jnp.arange(channels, dtype=jnp.int32)[None, :]
+    picked = jnp.dot(
+        picking.astype(traces.dtype), samples, preferred_element_type=jnp.float32
+    ).astype(traces.dtype)
+    swap = [(0, 1), (1, 0)]
+    kept = lax.dynamic_slice_in_dim(samples, seg * receivers, receivers, 0)
+    given = lax.dynamic_slice_in_dim(samples, (1 - seg) * receivers, receivers, 0)
+    taken = lax.ppermute(given, "seg", swap)
+    white = whitened_spectra(jnp.concatenate([kept, taken], axis=0), forward)
+    everyone = lax.all_gather(white.reshape(2, receivers, 2 * NF), "row", axis=0)
+    mine = lax.psum_scatter(picked, "row", scatter_dimension=0, tiled=True)
+    slots = mine.shape[0]
+    other = lax.ppermute(mine, "seg", swap)
+    white_sources = whitened_spectra(jnp.concatenate([mine, other], axis=0), forward)
+    return correlate_gathers(everyone, white_sources.reshape(2, slots, 2 * NF), back)
+
+
 def solution(mesh):
     placed = (P(("run", "seg"), "row", "col"), P(("run", "row")), P(), P())
+    body = local
+    if mesh.shape["col"] == 1 and mesh.shape["seg"] == 2:
+        forward, back = host_tables(NT)
+        body = partial(paired, forward, back)
     return jax.shard_map(
-        local,
+        body,
         mesh=mesh,
         in_specs=placed,
         out_specs=P(("run", "row"), None, ("col", "seg"), None),

time: 271 us -> 109 us (0.40)
  waiting for transfers between devices: 73.4 us -> 8.54 us
  matrix products: 70 us -> 9.97 us
  blocking collectives: 75.2 us -> 44.5 us
  other arithmetic: 17.9 us -> 3.12 us
  Pallas kernels: 0 us -> 14 us
  local copies, waits for them, and re-layouts: 16.3 us -> 4.79 us
  starting transfers between devices: 0.04 us -> 9.72 us
  loops' own time: 4.26 us -> 0 us
    all_to_all x1 -> x0, blocking collectives: 75.2 us -> none  [local(): lax.all_to_all(outgoing[:, None], 'row', split_axis=0, concat_axis=1, til...]
    dot_general x5 -> x3, matrix products: 70 us -> 9.97 us  [the longest x2 9.57 us: whitened_spectra(): spectra = jnp.dot(samples, forward, preferred_element_type=jnp.float32)]
    unnamed x0 -> x1, blocking collectives: none -> 44.5 us
    all_gather x1, waiting for transfers between devices: 43.1 us -> 0.02 us  [paired(): lax.all_gather(white.reshape(2, receivers, 2 * NF), 'row', axis=0)]
    reduce_scatter x1 -> x0, waiting for transfers between devices: 30.3 us -> none  [local(): lax.psum_scatter(blocks.reshape(receivers * lax.axis_size(('col', 'seg'))...]
    pallas_call x0 -> x1, Pallas kernels: none -> 14 us  [correlate_gathers(): pl.pallas_call(gather_kernel, grid=(blocks,), in_specs=[pl.BlockSpec((1,...]
    convert_element_type x8 -> x3, other arithmetic: 10.7 us -> 1.43 us  [the longest x2 0.77 us: whitened_spectra(): (spectra * jnp.concatenate([scaling, scaling], axis=1)).astype(jnp.bfloat16)]
    gather x2 -> x0, local copies, waits for them, and re-layouts: 7.05 us -> none  [the longest x1 3.52 us: local(): source_imag = jnp.take(everyone, real_cols + channels, axis=1)]
  transfers between devices with their start and end apart: 2 -> 7, of which waited for: 2 -> 3; matrix products, arithmetic and copies ran while one was open for 4% -> 48% of each run, Pallas kernels for 0% -> 0%
where the time goes in v1:
time: 109 us
  blocking collectives  44.5 us (41%)
  between operations  14.2 us (13%)
  Pallas kernels  14 us (13%)
  matrix products  9.97 us (9%)
  starting transfers between devices  9.72 us (9%)
  waiting for transfers between devices  8.54 us (8%)
  local copies, waits for them, and re-layouts  4.79 us (4%)
  other arithmetic  3.12 us (3%)
    unnamed x1, blocking collectives  44.5 us
    pallas_call x1, Pallas kernels, correlate_gathers(): pl.pallas_call(gather_kernel, grid=(blocks,), in_specs=[pl.BlockSpec((1,...  14 us
    dot_general x2, matrix products, whitened_spectra(): spectra = jnp.dot(samples, forward, preferred_element_type=jnp.float32)  9.57 us
    unnamed x4, starting transfers between devices  5.17 us
    unnamed x14, local copies, waits for them, and re-layouts  3.57 us
    ppermute x1, waiting for transfers between devices, paired(): taken = lax.ppermute(given, 'seg', swap)  3.5 us
    ppermute x1, starting transfers between devices, paired(): taken = lax.ppermute(given, 'seg', swap)  3 us
    ppermute x1, waiting for transfers between devices, paired(): other = lax.ppermute(mine, 'seg', swap)  2.79 us
  transfers between devices with their start and end apart: 7, of which 3 were waited for; matrix products, arithmetic and copies ran while one was open for 48% of the time, Pallas kernels for 0%

profile of v1, /device:TPU:0, one launch (start us, length us, event | category | flops | bytes accessed | tf_op | source)
XLA Modules:
  0.0 108.8 jit_solution(13517096766573931314)
XLA Ops:
  6.5 0.0 all-gather.2.cloned.1.call-start
  6.5 0.7 convert_element_type.16
  7.2 1.0 bitcast_multiply_fusion
  8.3 3.0 %collective-permute-start = (bf16[32,2048]{1,0:T(8,128)(2,1)S(1)}, bf16[32,2048]{1,0:T(8,128)(2,1)S(1)}, u32[]{:S(2)}, u32[]{:S(2)}) collective-permute-start(bf16[32,2048]{1,0:T(8,128)(2,1)S(1)} %get-tuple-element.6), channel_id=1, source_target_pairs={{0,1},{1,0},{2,3},{3,2},{4,5},{5,4},{6,7},{7,6},{8,9},{9,8},{10,11... | collective-permute-start | bytes 393224 | tf_op jit(solution)/shard_map/ppermute | solution.py:221
  11.3 3.5 %collective-permute-done = bf16[32,2048]{1,0:T(8,128)(2,1)S(1)} collective-permute-done((bf16[32,2048]{1,0:T(8,128)(2,1)S(1)}, bf16[32,2048]{1,0:T(8,128)(2,1)S(1)}, u32[]{:S(2)}, u32[]{:S(2)}) %collective-permute-start) | collective-permute-done | bytes 131104 | tf_op jit(solution)/shard_map/ppermute | solution.py:221
  14.8 0.0 copy-start.2
  14.8 0.0 copy-start.3
  14.8 0.0 copy-start.4
  14.8 5.0 %fusion.11 = (f32[64,2048]{1,0:T(8,128)S(1)}, f32[64,2048]{1,0:T(8,128)S(1)}) fusion(bf16[2048,2048]{1,0:T(8,128)(2,1)} %constant.38.clone, bf16[32,2048]{1,0:T(8,128)(2,1)S(1)} %collective-permute-done, bf16[32,2048]{1,0:T(8,128)(2,1)S(1)} %get-tuple-element.5), kind=kOutput, calls=%fused_computation.29 | convolution fusion | flops 537526272 | bytes 9699328 | tf_op jit(solution)/shard_map/dot_general | solution.py:142
  19.8 0.4 reshape.35
  20.2 0.2 reduce_sum.36
  20.4 0.0 copy-start.1
  20.5 0.2 broadcast_in_dim.16
  20.6 0.2 reshape.36
  20.8 0.8 fusion.1
  21.6 0.0 all-gather.2.cloned.1.call-update
  21.6 0.0 copy-done.2
  21.6 0.2 convert_reduce_fusion
  21.8 0.0 copy-done.3
  21.8 0.1 select_reduce_fusion
  21.9 0.4 convolution_convert_fusion
  22.3 44.5 %fusion = bf16[16,2048]{1,0:T(8,128)(2,1)S(1)} fusion(bf16[192,2048]{1,0:T(8,128)(2,1)S(1)} %convolution_convert_fusion), kind=kCustom, calls=%all-reduce-scatter | all-reduce-scatter fusion | flops 524289 | bytes 852480
  66.9 1.3 %collective-permute-start.4 = (bf16[16,2048]{1,0:T(8,128)(2,1)S(1)}, bf16[16,2048]{1,0:T(8,128)(2,1)S(1)}, u32[]{:S(2)}, u32[]{:S(2)}) collective-permute-start(bf16[16,2048]{1,0:T(8,128)(2,1)S(1)} %fusion), channel_id=1, source_target_pairs={{0,6},{2,8},{4,10},{6,12},{8,14},{10,16},{12,18},{14,20},{16,22},{... | collective-permute-start | bytes 196616
  68.2 1.3 %collective-permute-start.3 = (bf16[16,2048]{1,0:T(8,128)(2,1)S(1)}, bf16[16,2048]{1,0:T(8,128)(2,1)S(1)}, u32[]{:S(2)}, u32[]{:S(2)}) collective-permute-start(bf16[16,2048]{1,0:T(8,128)(2,1)S(1)} %fusion), channel_id=1, source_target_pairs={{0,4},{2,6},{4,8},{6,10},{8,12},{10,14},{12,16},{14,18},{16,20},{1... | collective-permute-start | bytes 196616
  69.5 1.3 %collective-permute-start.2 = (bf16[16,2048]{1,0:T(8,128)(2,1)S(1)}, bf16[16,2048]{1,0:T(8,128)(2,1)S(1)}, u32[]{:S(2)}, u32[]{:S(2)}) collective-permute-start(bf16[16,2048]{1,0:T(8,128)(2,1)S(1)} %fusion), channel_id=1, source_target_pairs={{0,2},{2,4},{4,6},{6,8},{8,10},{10,12},{12,14},{14,16},{16,18},{18... | collective-permute-start | bytes 196616
  70.8 1.3 %collective-permute-start.5 = (bf16[12,2048]{1,0:T(8,128)(2,1)S(1)}, bf16[12,2048]{1,0:T(8,128)(2,1)S(1)}, u32[]{:S(2)}, u32[]{:S(2)}) collective-permute-start(bf16[12,2048]{1,0:T(8,128)(2,1)S(1)} %slice), channel_id=1, source_target_pairs={{0,8},{2,10},{4,12},{6,14},{8,16},{10,18},{12,20},{14,22},{16,24},... | collective-permute-start | bytes 147464
  72.1 0.0 copy-done.4
  72.1 0.6 dynamic-slice.4
  73.2 2.2 %collective-permute-done.5 = bf16[12,2048]{1,0:T(8,128)(2,1)S(1)} collective-permute-done((bf16[12,2048]{1,0:T(8,128)(2,1)S(1)}, bf16[12,2048]{1,0:T(8,128)(2,1)S(1)}, u32[]{:S(2)}, u32[]{:S(2)}) %collective-permute-start.5) | collective-permute-done | bytes 49184
  75.4 0.0 collective-permute-done.4
  75.4 0.0 collective-permute-done.3
  75.4 0.0 collective-permute-done.2
  75.5 0.7 concatenate.16
  76.2 1.5 %collective-permute-start.1 = (bf16[12,2048]{1,0:T(8,128)(2,1)S(1)}, bf16[12,2048]{1,0:T(8,128)(2,1)S(1)}, u32[]{:S(2)}, u32[]{:S(2)}) collective-permute-start(bf16[12,2048]{1,0:T(8,128)(2,1)S(1)} %constant_dynamic-slice_fusion), channel_id=1, source_target_pairs={{0,1},{1,0},{2,3},{3,2},{4,5},{5,4},{6,7},{7,6},{8,9},{9,8},{10,11... | collective-permute-start | bytes 147464 | tf_op jit(solution)/shard_map/ppermute | solution.py:226
  77.8 2.8 %collective-permute-done.1 = bf16[12,2048]{1,0:T(8,128)(2,1)S(1)} collective-permute-done((bf16[12,2048]{1,0:T(8,128)(2,1)S(1)}, bf16[12,2048]{1,0:T(8,128)(2,1)S(1)}, u32[]{:S(2)}, u32[]{:S(2)}) %collective-permute-start.1) | collective-permute-done | bytes 49184 | tf_op jit(solution)/shard_map/ppermute | solution.py:226
  80.6 4.6 %fusion.12 = (f32[24,2048]{1,0:T(8,128)S(1)}, f32[24,2048]{1,0:T(8,128)S(1)}) fusion(bf16[2048,2048]{1,0:T(8,128)(2,1)} %constant.38.clone, bf16[12,2048]{1,0:T(8,128)(2,1)S(1)} %collective-permute-done.1, bf16[12,2048]{1,0:T(8,128)(2,1)S(1)} %constant_dynamic-slice_fusion), kind=kOutput, calls=%fused_computation.30 | convolution fusion | flops 201572352 | bytes 8880128 | tf_op jit(solution)/shard_map/dot_general | solution.py:142
  85.2 0.2 reshape.37
  85.3 0.1 reduce_sum.39
  85.5 0.1 broadcast_in_dim.29
  85.6 0.1 reshape.38
  85.8 0.0 all-gather.2.cloned.1.call-done.recv_ref
  85.8 0.0 copy-done.1
  85.8 0.0 copy-start
  85.8 2.2 %copy-done = bf16[16,2,32,2048]{3,2,1,0:T(8,128)(2,1)S(1)} copy-done((bf16[16,2,32,2048]{3,2,1,0:T(8,128)(2,1)S(1)}, bf16[16,2,32,2048]{3,2,1,0:T(8,128)(2,1)}, u32[]{:S(2)}) %copy-start) | copy-done | bytes 4194328
  88.0 14.0 %shard_map.64 = bf16[12,16,32,256]{3,2,1,0:T(8,128)(2,1)} custom-call(bf16[16,2,32,2048]{3,2,1,0:T(8,128)(2,1)S(1)} %copy-done, bf16[2,12,2048]{2,1,0:T(8,128)(2,1)S(1)} %reshape.39.source_ref, bf16[2048,256]{1,0:T(8,128)(2,1)S(1)} %copy-done.1), custom_call_target="tpu_custom_call" | custom-call | flops 6442450944 | bytes 7340032 | tf_op jit(solution)/shard_map/pallas_call | solution.py:175
  (10 shorter events, 0.2 us)
Async XLA Ops:
  6.5 79.3 %all-gather.2.cloned.1.call-start = ((), (), s32[]{:S(2)}) async-start(), calls=%async_computation | async-start | bytes 4456448 | tf_op jit(solution)/shard_map/all_gather | solution.py:223
  8.3 6.5 %collective-permute-start = (bf16[32,2048]{1,0:T(8,128)(2,1)S(1)}, bf16[32,2048]{1,0:T(8,128)(2,1)S(1)}, u32[]{:S(2)}, u32[]{:S(2)}) collective-permute-start(bf16[32,2048]{1,0:T(8,128)(2,1)S(1)} %get-tuple-element.6), channel_id=1, source_target_pairs={{0,1},{1,0},{2,3},{3,2},{4,5},{5,4},{6,7},{7,6},{8,9},{9,8},{10,11... | collective-permute-start | bytes 393224 | tf_op jit(solution)/shard_map/ppermute | solution.py:221
  14.8 6.8 %copy-start.2 = (s32[64,1]{0,1:T(1,128)S(1)}, s32[64,1]{0,1:T(1,128)}, u32[]{:S(2)}) copy-start(s32[64,1]{0,1:T(1,128)} %param.9) | copy-start | bytes 772
  14.8 7.0 %copy-start.3 = (s32[64]{0:T(128)S(1)}, s32[64]{0:T(128)}, u32[]{:S(2)}) copy-start(s32[64]{0:T(128)} %param.8) | copy-start | bytes 772
  14.8 57.3 %copy-start.4 = (u32[32]{0:T(128)S(1)}, u32[32]{0:T(128)}, u32[]{:S(2)}) copy-start(u32[32]{0:T(128)} %constant.43) | copy-start | bytes 388
  20.4 65.4 %copy-start.1 = (bf16[2048,256]{1,0:T(8,128)(2,1)S(1)}, bf16[2048,256]{1,0:T(8,128)(2,1)}, u32[]{:S(2)}) copy-start(bf16[2048,256]{1,0:T(8,128)(2,1)} %constant.39.clone.back_ref) | copy-start | bytes 3145732
  66.9 8.6 %collective-permute-start.4 = (bf16[16,2048]{1,0:T(8,128)(2,1)S(1)}, bf16[16,2048]{1,0:T(8,128)(2,1)S(1)}, u32[]{:S(2)}, u32[]{:S(2)}) collective-permute-start(bf16[16,2048]{1,0:T(8,128)(2,1)S(1)} %fusion), channel_id=1, source_target_pairs={{0,6},{2,8},{4,10},{6,12},{8,14},{10,16},{12,18},{14,20},{16,22},{... | collective-permute-start | bytes 196616
  68.2 7.3 %collective-permute-start.3 = (bf16[16,2048]{1,0:T(8,128)(2,1)S(1)}, bf16[16,2048]{1,0:T(8,128)(2,1)S(1)}, u32[]{:S(2)}, u32[]{:S(2)}) collective-permute-start(bf16[16,2048]{1,0:T(8,128)(2,1)S(1)} %fusion), channel_id=1, source_target_pairs={{0,4},{2,6},{4,8},{6,10},{8,12},{10,14},{12,16},{14,18},{16,20},{1... | collective-permute-start | bytes 196616
  69.5 6.0 %collective-permute-start.2 = (bf16[16,2048]{1,0:T(8,128)(2,1)S(1)}, bf16[16,2048]{1,0:T(8,128)(2,1)S(1)}, u32[]{:S(2)}, u32[]{:S(2)}) collective-permute-start(bf16[16,2048]{1,0:T(8,128)(2,1)S(1)} %fusion), channel_id=1, source_target_pairs={{0,2},{2,4},{4,6},{6,8},{8,10},{10,12},{12,14},{14,16},{16,18},{18... | collective-permute-start | bytes 196616
  70.8 4.7 %collective-permute-start.5 = (bf16[12,2048]{1,0:T(8,128)(2,1)S(1)}, bf16[12,2048]{1,0:T(8,128)(2,1)S(1)}, u32[]{:S(2)}, u32[]{:S(2)}) collective-permute-start(bf16[12,2048]{1,0:T(8,128)(2,1)S(1)} %slice), channel_id=1, source_target_pairs={{0,8},{2,10},{4,12},{6,14},{8,16},{10,18},{12,20},{14,22},{16,24},... | collective-permute-start | bytes 147464
  76.2 4.3 %collective-permute-start.1 = (bf16[12,2048]{1,0:T(8,128)(2,1)S(1)}, bf16[12,2048]{1,0:T(8,128)(2,1)S(1)}, u32[]{:S(2)}, u32[]{:S(2)}) collective-permute-start(bf16[12,2048]{1,0:T(8,128)(2,1)S(1)} %constant_dynamic-slice_fusion), channel_id=1, source_target_pairs={{0,1},{1,0},{2,3},{3,2},{4,5},{5,4},{6,7},{7,6},{8,9},{9,8},{10,11... | collective-permute-start | bytes 147464 | tf_op jit(solution)/shard_map/ppermute | solution.py:226
  85.8 2.2 %copy-start = (bf16[16,2,32,2048]{3,2,1,0:T(8,128)(2,1)S(1)}, bf16[16,2,32,2048]{3,2,1,0:T(8,128)(2,1)}, u32[]{:S(2)}) copy-start(bf16[16,2,32,2048]{3,2,1,0:T(8,128)(2,1)} %all-gather.2.cloned.1.call-done.recv_ref) | copy-start | bytes 12582916
Sparse Core Ops, SparseCore 0:
  21.7 54.6 all-gather.1

commit v2 on v0

--- a/solution.py
+++ b/solution.py
@@ -1,8 +1,12 @@
 import math
+from functools import partial
 
 import jax
 import jax.numpy as jnp
+import numpy as np
 from jax import lax
+from jax.experimental import pallas as pl
+from jax.experimental.pallas import tpu as pltpu
 from jax.sharding import PartitionSpec as P
 
 NT = 2048
@@ -122,10 +126,323 @@
     return lax.all_to_all(outgoing[:, None], "row", split_axis=0, concat_axis=1, tiled=True)
 
 
+def host_tables(num_samples):
+    samples = np.arange(num_samples, dtype=np.int64)
+    bins = np.arange(NF, dtype=np.int64)
+    angles = (samples[:, None] * bins[None, :] % NT) * (two_pi / NT)
+    forward = np.concatenate([np.cos(angles), -np.sin(angles)], axis=1)
+    lags = np.arange(LAGS, dtype=np.int64) - LAGS // 2 + NT
+    lag_angles = (bins[:, None] * lags[None, :] % NT) * (two_pi / NT)
+    back = np.concatenate([np.cos(lag_angles), -np.sin(lag_angles)], axis=0)
+    return forward.astype(jnp.bfloat16), back.astype(jnp.bfloat16)
+
+
+def at_ring(place, lines):
+    second = place // lines
+    return second, (1 - second) * place + second * (2 * lines - 1 - place)
+
+
+def fused_kernel(
+    chips, slots, traces_ref, live_ref, picking_ref, choose_ref, forward_hbm, back_ref, out_ref,
+    forward, samples, given_in, picked, core_in, part, parts_in, chosen, white_source, everyone,
+    cross, table_sem, pair_send, pair_recv, deal_send, deal_recv, share_send, share_recv,
+    right_send, right_recv, left_send, left_recv, twin_send, twin_recv,
+):
+    lines = chips // 2
+    half = chips // 2
+    row = lax.axis_index("row")
+    seg = lax.axis_index("seg")
+    chip, core = row // 2, row % 2
+    line, side = chip // 2, chip % 2
+    place = (1 - side) * line + side * (2 * lines - 1 - line)
+    channels, width = traces_ref.shape
+    receivers = channels // 2
+    own_sources = picking_ref.shape[0] // 2
+    columns = width // chips
+
+    def chip_at(where):
+        second, first = at_ring((where + chips) % chips, lines)
+        return first * 2 + second
+
+    def remote(source, target, send_sem, recv_sem, peer):
+        return pltpu.make_async_remote_copy(
+            src_ref=source, dst_ref=target, send_sem=send_sem, recv_sem=recv_sem,
+            device_id=peer, device_id_type=pl.DeviceIdType.MESH,
+        )
+
+    table_copy = pltpu.make_async_copy(forward_hbm, forward, table_sem)
+    table_copy.start()
+    twin = {"row": chip * 2 + 1 - core}
+    across = {"seg": 1 - seg}
+    peers = [{"row": (chip + step) % chips * 2 + core} for step in range(1, chips)]
+    barrier = pltpu.get_barrier_semaphore()
+    for peer in [twin, across] + peers:
+        pl.semaphore_signal(barrier, inc=1, device_id=peer, device_id_type=pl.DeviceIdType.MESH)
+
+    samples[...] = traces_ref[...] * live_ref[...]
+    picked[...] = jnp.dot(
+        picking_ref[...], samples[...], preferred_element_type=jnp.float32
+    ).astype(picked.dtype)
+    pl.semaphore_wait(barrier, chips + 1)
+
+    def rows_of(first, count):
+        return pl.ds(pl.multiple_of(first, count), count)
+
+    my_rows = rows_of(core * own_sources, own_sources)
+    twin_rows = rows_of((1 - core) * own_sources, own_sources)
+    swap = remote(
+        samples.at[rows_of((1 - seg) * receivers, receivers)], given_in,
+        pair_send.at[0], pair_recv.at[0], across,
+    )
+    fold = remote(picked.at[twin_rows], core_in, pair_send.at[1], pair_recv.at[1], twin)
+    fold.start()
+    swap.start()
+
+    def columns_of(which):
+        return pl.ds(pl.multiple_of(which * columns, columns), columns)
+
+    fold.wait_recv()
+    part[...] = picked[my_rows, :] + core_in[...]
+    deals = []
+    for step, peer in enumerate(peers):
+        deals.append(remote(
+            part.at[:, columns_of((chip + step + 1) % chips)], parts_in.at[step],
+            deal_send.at[step], deal_recv.at[step], peer,
+        ))
+    for copy in deals:
+        copy.start()
+
+    def whiten(traces):
+        count = traces.shape[0]
+        real = jnp.dot(traces, forward[:, :NF], preferred_element_type=jnp.float32)
+        imag = jnp.dot(traces, forward[:, NF:], preferred_element_type=jnp.float32)
+        first = lax.broadcasted_iota(jnp.int32, (2 * BAND, 2 * BAND), 0) // BAND
+        second = lax.broadcasted_iota(jnp.int32, (2 * BAND, 2 * BAND), 1) // BAND
+        same = jnp.where(first == second, 1.0, 0.0).astype(jnp.bfloat16)
+        power = real * real + imag * imag
+        scales = []
+        for low in range(0, NF, 2 * BAND):
+            piece = power[:, low : low + 2 * BAND]
+            upper = piece.astype(jnp.bfloat16)
+            lower = (piece - upper.astype(jnp.float32)).astype(jnp.bfloat16)
+            total = jnp.dot(upper, same, preferred_element_type=jnp.float32) + jnp.dot(
+                lower, same, preferred_element_type=jnp.float32
+            )
+            scales.append(lax.rsqrt(total / (2 * BAND) + 1e-05))
+        scaling = jnp.concatenate(scales, axis=1)
+        return (real * scaling).astype(jnp.bfloat16), (imag * scaling).astype(jnp.bfloat16)
+
+    table_copy.wait()
+    swap.wait_recv()
+    kept = samples[rows_of(seg * receivers, receivers), :]
+    real, imag = whiten(jnp.concatenate([kept, given_in[...]], axis=0))
+    everyone[row, :, :NF] = real
+    everyone[row, :, NF:] = imag
+
+    def shard(where, stream, piece):
+        return everyone.at[chip_at(where) * 2 + stream, pl.ds(piece * receivers, receivers)]
+
+    right_peer = {"row": chip_at(place + 1) * 2 + core}
+    left_peer = {"row": chip_at(place - 1) * 2 + core}
+
+    def right(hop, piece):
+        index = (hop - 1) * 2 + piece
+        block = shard(place - hop + 1, core, piece)
+        return remote(block, block, right_send.at[index], right_recv.at[index], right_peer)
+
+    def left(hop, piece):
+        index = (hop - 1) * 2 + piece
+        block = shard(place + hop - 1, core, piece)
+        return remote(block, block, left_send.at[index], left_recv.at[index], left_peer)
+
+    order = [0]
+    for hop in range(1, half):
+        order += [-hop, hop]
+    order.append(-half)
+
+    def to_twin(number, piece):
+        index = number * 2 + piece
+        block = shard(place + order[number], core, piece)
+        return remote(block, block, twin_send.at[index], twin_recv.at[index], twin)
+
+    started = []
+
+    def go(copy):
+        copy.start()
+        started.append(copy)
+
+    for piece in range(2):
+        go(right(1, piece))
+        go(left(1, piece))
+    for piece in range(2):
+        go(to_twin(0, piece))
+
+    for copy in deals:
+        copy.wait_recv()
+    total = part[:, columns_of(chip)].astype(jnp.float32)
+    for step in range(chips - 1):
+        total = total + parts_in[step].astype(jnp.float32)
+    chosen[0, my_rows, columns_of(chip)] = total.astype(chosen.dtype)
+    mine = chosen.at[0, my_rows, columns_of(chip)]
+    shares = [
+        remote(mine, mine, share_send.at[step], share_recv.at[step], peer)
+        for step, peer in enumerate(peers)
+    ]
+    for copy in shares:
+        copy.start()
+    for copy in shares:
+        copy.wait_recv()
+    over = remote(
+        chosen.at[0, my_rows], chosen.at[1, my_rows], pair_send.at[2], pair_recv.at[2], across
+    )
+    over.start()
+    here = remote(
+        chosen.at[0, my_rows], chosen.at[0, my_rows], pair_send.at[3], pair_recv.at[3], twin
+    )
+    here.start()
+
+    def event(hop, piece):
+        if hop < half or piece == 0:
+            right(hop, piece).wait_recv()
+            if hop + 1 < half or (hop + 1 == half and piece == 0):
+                go(right(hop + 1, piece))
+            go(to_twin(2 * hop - 1, piece))
+        if hop < half or piece == 1:
+            left(hop, piece).wait_recv()
+            if hop + 1 < half or (hop + 1 == half and piece == 1):
+                go(left(hop + 1, piece))
+            go(to_twin(2 * hop if hop < half else 2 * hop - 1, piece))
+
+    event(1, 0)
+    over.wait_recv()
+    there = remote(
+        chosen.at[1, my_rows], chosen.at[1, my_rows], pair_send.at[4], pair_recv.at[4], twin
+    )
+    there.start()
+    event(1, 1)
+    here.wait_recv()
+    there.wait_recv()
+    choose = choose_ref[...]
+    own = jnp.concatenate(
+        [
+            jnp.dot(choose, chosen[which], preferred_element_type=jnp.float32).astype(jnp.bfloat16)
+            for which in range(2)
+        ],
+        axis=0,
+    )
+    real, imag = whiten(own)
+    white_source[:, :NF] = real
+    white_source[:, NF:] = imag
+    padded = choose_ref.shape[0]
+
+    def correlate_chip(number):
+        for piece in range(2):
+            to_twin(number, piece).wait_recv()
+        where = chip_at(place + order[number])
+
+        @pl.loop(0, 2)
+        def _(stream):
+            block = where * 2 + stream
+            for slot in range(slots):
+                cross_real = cross_imag = None
+                for which in range(2):
+                    rows = pl.ds(which * receivers, receivers)
+                    recv_real = everyone[block, rows, :NF]
+                    recv_imag = everyone[block, rows, NF:]
+                    at = which * padded + slot
+                    source_real = white_source[at : at + 1, :NF]
+                    source_imag = white_source[at : at + 1, NF:]
+                    term_real = source_real * recv_real + source_imag * recv_imag
+                    term_imag = source_imag * recv_real - source_real * recv_imag
+                    cross_real = term_real if cross_real is None else cross_real + term_real
+                    cross_imag = term_imag if cross_imag is None else cross_imag + term_imag
+                cross[slot * receivers : (slot + 1) * receivers, :NF] = cross_real
+                cross[slot * receivers : (slot + 1) * receivers, NF:] = cross_imag
+            stacked = jnp.dot(cross[...], back_ref[...], preferred_element_type=jnp.float32)
+            mean_sq = jnp.mean(stacked * stacked, axis=-1, keepdims=True)
+            normed = (stacked * lax.rsqrt(mean_sq + 1e-06)).astype(out_ref.dtype)
+            for slot in range(slots):
+                out_ref[slot, block] = normed[slot * receivers : (slot + 1) * receivers]
+
+    number = 0
+    for hop in range(2, half + 1):
+        for piece in range(2):
+            event(hop, piece)
+            correlate_chip(number)
+            number += 1
+    while number < chips:
+        correlate_chip(number)
+        number += 1
+    for copy in deals + shares + started + [swap, fold, over, here, there]:
+        copy.wait_send()
+
+
+def paired(forward, back, traces, live_mask, sources, owners):
+    row_count = lax.axis_size("row")
+    row = lax.axis_index("row")
+    chips = row_count // 2
+    channels, width = traces.shape[1:]
+    receivers = channels // 2
+    num_sources = sources.shape[0]
+    slots = 3 * num_sources // row_count
+    padded = -(-slots // 16) * 16
+    owner_ids = owners[:, 0]
+    order_ids = jnp.arange(num_sources, dtype=jnp.int32)
+    earlier = (owner_ids[:, None] == owner_ids[None, :]) & (order_ids[None, :] < order_ids[:, None])
+    rank = jnp.sum(earlier.astype(jnp.int32), axis=1)
+    slot_of = jnp.where(owner_ids == row, rank, padded)
+    choose = jnp.arange(padded, dtype=jnp.int32)[:, None] == slot_of[None, :]
+    local_ids = row * channels + jnp.arange(channels, dtype=jnp.int32)
+    picking = sources[:, None] == local_ids[None, :]
+    kind = traces.dtype
+    whole = pl.BlockSpec(memory_space=pltpu.VMEM)
+    dma = pltpu.SemaphoreType.DMA
+    hops = chips // 2 * 2
+    return pl.pallas_call(
+        partial(fused_kernel, chips, slots),
+        in_specs=[whole] * 4 + [pl.BlockSpec(memory_space=pl.ANY), whole],
+        out_specs=whole,
+        out_shape=jax.ShapeDtypeStruct((slots, row_count, receivers, LAGS), jnp.bfloat16),
+        scratch_shapes=[
+            pltpu.VMEM(forward.shape, kind),
+            pltpu.VMEM((channels, width), kind),
+            pltpu.VMEM((receivers, width), kind),
+            pltpu.VMEM((num_sources, width), kind),
+            pltpu.VMEM((num_sources // 2, width), kind),
+            pltpu.VMEM((num_sources // 2, width), kind),
+            pltpu.VMEM((chips - 1, num_sources // 2, width // chips), kind),
+            pltpu.VMEM((2, num_sources, width), kind),
+            pltpu.VMEM((2 * padded, 2 * NF), kind),
+            pltpu.VMEM((row_count, channels, 2 * NF), kind),
+            pltpu.VMEM((slots * receivers, 2 * NF), kind),
+            dma,
+            dma((5,)), dma((5,)),
+            dma((chips - 1,)), dma((chips - 1,)),
+            dma((chips - 1,)), dma((chips - 1,)),
+            dma((hops,)), dma((hops,)),
+            dma((hops,)), dma((hops,)),
+            dma((2 * chips,)), dma((2 * chips,)),
+        ],
+        compiler_params=pltpu.CompilerParams(
+            collective_id=0, has_side_effects=True, vmem_limit_bytes=56 << 20
+        ),
+        cost_estimate=pl.CostEstimate(
+            flops=2 * slots * row_count * receivers * 2 * NF * LAGS,
+            bytes_accessed=2 * width * 2 * NF,
+            transcendentals=0,
+        ),
+    )(traces[0], live_mask.astype(kind)[:, None], picking.astype(kind), choose.astype(kind),
+      forward, back)
+
+
 def solution(mesh):
     placed = (P(("run", "seg"), "row", "col"), P(("run", "row")), P(), P())
+    body = local
+    if mesh.shape["col"] == 1 and mesh.shape["seg"] == 2 and mesh.shape["row"] % 4 == 0:
+        forward, back = host_tables(NT)
+        body = partial(paired, forward, back)
     return jax.shard_map(
-        local,
+        body,
         mesh=mesh,
         in_specs=placed,
         out_specs=P(("run", "row"), None, ("col", "seg"), None),

time: 271 us -> 57.7 us (0.21)
  blocking collectives: 75.2 us -> 0 us
  waiting for transfers between devices: 73.4 us -> 0 us
  matrix products: 70 us -> 0 us
  Pallas kernels: 0 us -> 48.8 us
  other arithmetic: 17.9 us -> 4.15 us
  between operations: 13.6 us -> 0.02 us
  local copies, waits for them, and re-layouts: 16.3 us -> 4.57 us
  loops' own time: 4.26 us -> 0 us
    all_to_all x1 -> x0, blocking collectives: 75.2 us -> none  [local(): lax.all_to_all(outgoing[:, None], 'row', split_axis=0, concat_axis=1, til...]
    dot_general x5 -> x0, matrix products: 70 us -> none  [the longest x1 31.3 us: local(): jnp.einsum('tf,ct->fc', sine_table, samples, preferred_element_type=jnp.f...]
    pallas_call x0 -> x1, Pallas kernels: none -> 48.8 us  [paired(): pl.pallas_call(partial(fused_kernel, chips, slots), in_specs=[whole] * 4...]
    all_gather x1 -> x0, waiting for transfers between devices: 43.1 us -> none  [local(): everyone = lax.all_gather(whitened, 'row', axis=1, tiled=True)]
    reduce_scatter x1 -> x0, waiting for transfers between devices: 30.3 us -> none  [local(): lax.psum_scatter(blocks.reshape(receivers * lax.axis_size(('col', 'seg'))...]
    convert_element_type x8 -> x2, other arithmetic: 10.7 us -> 1.92 us  [the longest x1 1.33 us: paired(): picking.astype(kind)]
    gather x2 -> x0, local copies, waits for them, and re-layouts: 7.05 us -> none  [the longest x1 3.52 us: local(): source_imag = jnp.take(everyone, real_cols + channels, axis=1)]
    another operation x1 -> x0, loops' own time: 4.26 us -> none  [local(): blocks = lax.map(one_group, offsets)]
  transfers between devices with their start and end apart: 2 -> 0, of which waited for: 2 -> 0; matrix products, arithmetic and copies ran while one was open for 4% -> 0% of each run, Pallas kernels for 0% -> 0%
where the time goes in v2:
time: 57.7 us; the launch traced here: 57.5 us
  Pallas kernels  48.8 us (85%)
  local copies, waits for them, and re-layouts  4.57 us (8%)
  other arithmetic  4.15 us (7%)
    pallas_call x1, Pallas kernels, paired(): pl.pallas_call(partial(fused_kernel, chips, slots), in_specs=[whole] * 4...  48.8 us
    unnamed x1, local copies, waits for them, and re-layouts  3.86 us
    convert_element_type x1, other arithmetic, paired(): picking.astype(kind)  1.33 us

profile of v2, /device:TPU:0, one launch (start us, length us, event | category | flops | bytes accessed | tf_op | source)
XLA Modules:
  0.0 57.5 jit_solution(2863748716349281666)
XLA Ops:
  0.0 0.7 %convert_bitcast_fusion = bf16[64,1]{0,1:T(2,128)(2,1)S(1)} fusion(s32[64]{0:T(128)} %param.7), kind=kLoop, calls=%fused_computation.8 | loop fusion | flops 64 | bytes 384 | tf_op jit(solution)/shard_map/broadcast_in_dim | solution.py:434
  0.7 0.9 %convert_reduce_fusion = s32[64]{0:T(128)S(1)} fusion(s32[64]{0:T(128)} %bitcast.5), kind=kLoop, calls=%fused_computation | loop fusion | flops 20416 | bytes 512 | tf_op jit(solution)/shard_map/reduce_sum | solution.py:392
  1.6 0.7 %compare_select_fusion = s32[64]{0:T(128)S(1)} fusion(s32[64]{0:T(128)S(1)} %convert_reduce_fusion, s32[]{:T(128)S(6)} %axis_index.15, s32[64,1]{0,1:T(1,128)} %param.9), kind=kLoop, calls=%fused_computation.6 | loop fusion | flops 128 | bytes 772 | tf_op jit(solution)/shard_map/jit(_where)/select_n | solution.py:393
  2.2 0.6 %fusion.1.choose_ref = bf16[16,64]{1,0:T(8,128)(2,1)} fusion(s32[64]{0:T(128)S(1)} %compare_select_fusion), kind=kLoop, calls=%fused_computation.5 | loop fusion | flops 2048 | bytes 2304 | tf_op jit(solution)/shard_map/convert_element_type | solution.py:434
  2.8 0.7 %copy.8.live_ref = bf16[64,1]{1,0:T(8,128)(2,1)} copy(bf16[64,1]{0,1:T(2,128)(2,1)S(1)} %convert_bitcast_fusion) | data formatting | bytes 256 | tf_op jit(solution)/shard_map/broadcast_in_dim | solution.py:434
  3.5 1.3 %compare_convert_fusion.picking_ref = bf16[64,64]{1,0:T(8,128)(2,1)} fusion(s32[64]{0:T(128)S(1)} %iota_add_fusion, s32[64]{0:T(128)} %param.8), kind=kLoop, calls=%fused_computation.3 | loop fusion | flops 8192 | bytes 8704 | tf_op jit(solution)/shard_map/convert_element_type | solution.py:434
  4.9 48.8 %shard_map.64 = bf16[12,16,32,256]{3,2,1,0:T(8,128)(2,1)} custom-call(bf16[64,2048]{1,0:T(8,128)(2,1)} %bitcast.6, bf16[64,1]{1,0:T(8,128)(2,1)} %copy.8.live_ref, bf16[64,64]{1,0:T(8,128)(2,1)} %compare_convert_fusion.picking_ref, bf16[16,64]{1,0:T(8,128)(2,1)} %fusion.1.choose_ref, bf16[2048,2048]{1,0:T(8,128)(2,1)} %constant.16.clone.forward_hbm, ...), custom_call_target="tpu_custom_call" | custom-call | flops 6442450944 | bytes 8388608 | tf_op jit(solution)/shard_map/pallas_call | solution.py:401
  53.7 3.9 %copy.10 = bf16[12,16,32,256]{3,2,1,0:T(8,128)(2,1)} copy(bf16[12,16,32,256]{3,2,1,0:T(8,128)(2,1)} %shard_map.64) | data formatting | bytes 6291456
  (1 shorter events, 0.0 us)

commit v3 on v2

--- a/solution.py
+++ b/solution.py
@@ -143,9 +143,9 @@
 
 
 def fused_kernel(
-    chips, slots, traces_ref, live_ref, picking_ref, choose_ref, forward_hbm, back_ref, out_ref,
+    chips, slots, traces_ref, live_ref, sources_ref, owners_ref, forward_hbm, back_ref, out_hbm,
     forward, samples, given_in, picked, core_in, part, parts_in, chosen, white_source, everyone,
-    cross, table_sem, pair_send, pair_recv, deal_send, deal_recv, share_send, share_recv,
+    cross_even, cross_odd, finished, table_sem, out_sem, pair_send, pair_recv, deal_send, deal_recv, share_send, share_recv,
     right_send, right_recv, left_send, left_recv, twin_send, twin_recv,
 ):
     lines = chips // 2
@@ -157,7 +157,9 @@
     place = (1 - side) * line + side * (2 * lines - 1 - line)
     channels, width = traces_ref.shape
     receivers = channels // 2
-    own_sources = picking_ref.shape[0] // 2
+    num_sources = sources_ref.shape[1]
+    own_sources = num_sources // 2
+    padded = white_source.shape[0] // 2
     columns = width // chips
 
     def chip_at(where):
@@ -179,10 +181,30 @@
     for peer in [twin, across] + peers:
         pl.semaphore_signal(barrier, inc=1, device_id=peer, device_id_type=pl.DeviceIdType.MESH)
 
-    samples[...] = traces_ref[...] * live_ref[...]
+    def ids(shape, axis):
+        return lax.broadcasted_iota(jnp.int32, shape, axis).astype(jnp.float32)
+
+    def column(values):
+        square = (values.shape[1], values.shape[1])
+        kept_ones = jnp.where(ids(square, 0) == ids(square, 1), values, 0.0)
+        return jnp.sum(kept_ones, axis=1, keepdims=True)
+
+    live = live_ref[...].astype(jnp.float32)
+    source_row = sources_ref[...].astype(jnp.float32)
+    owner_row = owners_ref[...].astype(jnp.float32)
+    my_row = row.astype(jnp.float32)
+    samples[...] = traces_ref[...] * column(live).astype(traces_ref.dtype)
+    local_ids = ids((num_sources, channels), 1) + my_row * channels
+    picking = jnp.where(column(source_row) == local_ids, 1.0, 0.0).astype(samples.dtype)
     picked[...] = jnp.dot(
-        picking_ref[...], samples[...], preferred_element_type=jnp.float32
+        picking, samples[...], preferred_element_type=jnp.float32
     ).astype(picked.dtype)
+    square = (num_sources, num_sources)
+    earlier = jnp.where(ids(square, 0) < ids(square, 1), 1.0, 0.0)
+    alike = jnp.where(column(owner_row) == owner_row, earlier, 0.0)
+    rank = jnp.sum(alike, axis=0, keepdims=True)
+    slot_of = jnp.where(owner_row == my_row, rank, float(padded))
+    choose = jnp.where(ids((padded, num_sources), 0) == slot_of, 1.0, 0.0).astype(samples.dtype)
     pl.semaphore_wait(barrier, chips + 1)
 
     def rows_of(first, count):
@@ -314,15 +336,15 @@
             go(to_twin(2 * hop if hop < half else 2 * hop - 1, piece))
 
     event(1, 0)
+    event(1, 1)
     over.wait_recv()
     there = remote(
         chosen.at[1, my_rows], chosen.at[1, my_rows], pair_send.at[4], pair_recv.at[4], twin
     )
     there.start()
-    event(1, 1)
     here.wait_recv()
+    event(2, 0)
     there.wait_recv()
-    choose = choose_ref[...]
     own = jnp.concatenate(
         [
             jnp.dot(choose, chosen[which], preferred_element_type=jnp.float32).astype(jnp.bfloat16)
@@ -333,39 +355,55 @@
     real, imag = whiten(own)
     white_source[:, :NF] = real
     white_source[:, NF:] = imag
-    padded = choose_ref.shape[0]
+
+    def cross_block(block, cross):
+        for slot in range(slots):
+            cross_real = cross_imag = None
+            for which in range(2):
+                rows = pl.ds(which * receivers, receivers)
+                recv_real = everyone[block, rows, :NF]
+                recv_imag = everyone[block, rows, NF:]
+                at = which * padded + slot
+                source_real = white_source[at : at + 1, :NF]
+                source_imag = white_source[at : at + 1, NF:]
+                term_real = source_real * recv_real + source_imag * recv_imag
+                term_imag = source_imag * recv_real - source_real * recv_imag
+                cross_real = term_real if cross_real is None else cross_real + term_real
+                cross_imag = term_imag if cross_imag is None else cross_imag + term_imag
+            cross[slot * receivers : (slot + 1) * receivers, :NF] = cross_real
+            cross[slot * receivers : (slot + 1) * receivers, NF:] = cross_imag
+
+    def finish_block(block, cross, index):
+        stacked = jnp.dot(cross[...], back_ref[...], preferred_element_type=jnp.float32)
+        mean_sq = jnp.mean(stacked * stacked, axis=-1, keepdims=True)
+        normed = (stacked * lax.rsqrt(mean_sq + 1e-06)).astype(finished.dtype)
+        for slot in range(slots):
+            finished[block, slot] = normed[slot * receivers : (slot + 1) * receivers]
+        copy = pltpu.make_async_copy(finished.at[block], out_hbm.at[:, block], out_sem.at[index])
+        copy.start()
+        written.append(copy)
+
+    written = []
+    waiting = []
+
+    def finish_waiting():
+        while waiting:
+            finish_block(*waiting.pop())
 
     def correlate_chip(number):
         for piece in range(2):
             to_twin(number, piece).wait_recv()
         where = chip_at(place + order[number])
-
-        @pl.loop(0, 2)
-        def _(stream):
+        for stream, cross in enumerate((cross_even, cross_odd)):
             block = where * 2 + stream
-            for slot in range(slots):
-                cross_real = cross_imag = None
-                for which in range(2):
-                    rows = pl.ds(which * receivers, receivers)
-                    recv_real = everyone[block, rows, :NF]
-                    recv_imag = everyone[block, rows, NF:]
-                    at = which * padded + slot
-                    source_real = white_source[at : at + 1, :NF]
-                    source_imag = white_source[at : at + 1, NF:]
-                    term_real = source_real * recv_real + source_imag * recv_imag
-                    term_imag = source_imag * recv_real - source_real * recv_imag
-                    cross_real = term_real if cross_real is None else cross_real + term_real
-                    cross_imag = term_imag if cross_imag is None else cross_imag + term_imag
-                cross[slot * receivers : (slot + 1) * receivers, :NF] = cross_real
-                cross[slot * receivers : (slot + 1) * receivers, NF:] = cross_imag
-            stacked = jnp.dot(cross[...], back_ref[...], preferred_element_type=jnp.float32)
-            mean_sq = jnp.mean(stacked * stacked, axis=-1, keepdims=True)
-            normed = (stacked * lax.rsqrt(mean_sq + 1e-06)).astype(out_ref.dtype)
-            for slot in range(slots):
-                out_ref[slot, block] = normed[slot * receivers : (slot + 1) * receivers]
-
-    number = 0
-    for hop in range(2, half + 1):
+            finish_waiting()
+            cross_block(block, cross)
+            waiting.append((block, cross, number * 2 + stream))
+
+    event(2, 1)
+    correlate_chip(0)
+    number = 1
+    for hop in range(3, half + 1):
         for piece in range(2):
             event(hop, piece)
             correlate_chip(number)
@@ -373,35 +411,29 @@
     while number < chips:
         correlate_chip(number)
         number += 1
+    finish_waiting()
     for copy in deals + shares + started + [swap, fold, over, here, there]:
         copy.wait_send()
+    for copy in written:
+        copy.wait()
 
 
 def paired(forward, back, traces, live_mask, sources, owners):
     row_count = lax.axis_size("row")
-    row = lax.axis_index("row")
     chips = row_count // 2
     channels, width = traces.shape[1:]
     receivers = channels // 2
     num_sources = sources.shape[0]
     slots = 3 * num_sources // row_count
     padded = -(-slots // 16) * 16
-    owner_ids = owners[:, 0]
-    order_ids = jnp.arange(num_sources, dtype=jnp.int32)
-    earlier = (owner_ids[:, None] == owner_ids[None, :]) & (order_ids[None, :] < order_ids[:, None])
-    rank = jnp.sum(earlier.astype(jnp.int32), axis=1)
-    slot_of = jnp.where(owner_ids == row, rank, padded)
-    choose = jnp.arange(padded, dtype=jnp.int32)[:, None] == slot_of[None, :]
-    local_ids = row * channels + jnp.arange(channels, dtype=jnp.int32)
-    picking = sources[:, None] == local_ids[None, :]
     kind = traces.dtype
     whole = pl.BlockSpec(memory_space=pltpu.VMEM)
     dma = pltpu.SemaphoreType.DMA
     hops = chips // 2 * 2
     return pl.pallas_call(
         partial(fused_kernel, chips, slots),
-        in_specs=[whole] * 4 + [pl.BlockSpec(memory_space=pl.ANY), whole],
-        out_specs=whole,
+        in_specs=[whole] * 4 + [pl.BlockSpec(memory_space=pltpu.HBM), whole],
+        out_specs=pl.BlockSpec(memory_space=pl.ANY),
         out_shape=jax.ShapeDtypeStruct((slots, row_count, receivers, LAGS), jnp.bfloat16),
         scratch_shapes=[
             pltpu.VMEM(forward.shape, kind),
@@ -415,7 +447,10 @@
             pltpu.VMEM((2 * padded, 2 * NF), kind),
             pltpu.VMEM((row_count, channels, 2 * NF), kind),
             pltpu.VMEM((slots * receivers, 2 * NF), kind),
+            pltpu.VMEM((slots * receivers, 2 * NF), kind),
+            pltpu.VMEM((row_count, slots, receivers, LAGS), kind),
             dma,
+            dma((row_count,)),
             dma((5,)), dma((5,)),
             dma((chips - 1,)), dma((chips - 1,)),
             dma((chips - 1,)), dma((chips - 1,)),
@@ -424,15 +459,14 @@
             dma((2 * chips,)), dma((2 * chips,)),
         ],
         compiler_params=pltpu.CompilerParams(
-            collective_id=0, has_side_effects=True, vmem_limit_bytes=56 << 20
+            collective_id=0, has_side_effects=True, vmem_limit_bytes=30 << 20
         ),
         cost_estimate=pl.CostEstimate(
             flops=2 * slots * row_count * receivers * 2 * NF * LAGS,
             bytes_accessed=2 * width * 2 * NF,
             transcendentals=0,
         ),
-    )(traces[0], live_mask.astype(kind)[:, None], picking.astype(kind), choose.astype(kind),
-      forward, back)
+    )(traces[0], live_mask[None, :], sources[None, :], owners.reshape(1, num_sources), forward, back)
 
 
 def solution(mesh):

time: 57.7 us -> 63.3 us (1.097)
  Pallas kernels: 48.8 us -> 53.8 us
  local copies, waits for them, and re-layouts: 4.57 us -> 9.19 us
  other arithmetic: 4.15 us -> 0 us
    unnamed x1 -> x13, local copies, waits for them, and re-layouts: 3.86 us -> 9.19 us
    pallas_call x1, Pallas kernels: 48.8 us -> 53.8 us  [paired(): pl.pallas_call(partial(fused_kernel, chips, slots), in_specs=[whole] * 4...]
    convert_element_type x2 -> x0, other arithmetic: 1.92 us -> none  [the longest x1 1.33 us: paired(): picking.astype(kind)]
    reduce_sum x1 -> x0, other arithmetic: 0.91 us -> none  [paired(): rank = jnp.sum(earlier.astype(jnp.int32), axis=1)]
    broadcast_in_dim x1 -> x0, local copies, waits for them, and re-layouts: 0.71 us -> none  [paired(): live_mask.astype(kind)[:, None]]
    select_n x1 -> x0, other arithmetic: 0.67 us -> none  [paired(): slot_of = jnp.where(owner_ids == row, rank, padded)]
    broadcast_in_dim x1 -> x0, other arithmetic: 0.66 us -> none  [paired(): live_mask.astype(kind)[:, None]]
where the time goes in v3:
time: 63.3 us; the launch traced here: 63 us
  Pallas kernels  53.8 us (85%)
  local copies, waits for them, and re-layouts  9.19 us (15%)
    pallas_call x1, Pallas kernels, paired(): pl.pallas_call(partial(fused_kernel, chips, slots), in_specs=[whole] * 4...  53.8 us
    unnamed x13, local copies, waits for them, and re-layouts  9.19 us

profile of v3, /device:TPU:0, one launch (start us, length us, event | category | flops | bytes accessed | tf_op | source)
XLA Modules:
  0.0 63.0 jit_solution(11701068960801332835)
XLA Ops:
  0.0 0.0 copy-start
  0.0 0.9 %copy-done = bf16[1,64,2048]{2,1,0:T(8,128)(2,1)S(1)} copy-done((bf16[1,64,2048]{2,1,0:T(8,128)(2,1)S(1)}, bf16[1,64,2048]{2,1,0:T(8,128)(2,1)}, u32[]{:S(2)}) %copy-start) | copy-done | bytes 262168
  1.0 0.0 copy-start.1
  1.0 0.7 %copy-done.1 = s32[64]{0:T(128)S(1)} copy-done((s32[64]{0:T(128)S(1)}, s32[64]{0:T(128)}, u32[]{:S(2)}) %copy-start.1) | copy-done | bytes 280
  1.6 0.0 copy-start.2
  1.6 0.7 %copy-done.2 = s32[64]{0:T(128)S(1)} copy-done((s32[64]{0:T(128)S(1)}, s32[64]{0:T(128)}, u32[]{:S(2)}) %copy-start.2) | copy-done | bytes 280
  2.3 0.0 copy-start.3
  2.3 0.7 %copy-done.3 = s32[64,1]{0,1:T(1,128)S(1)} copy-done((s32[64,1]{0,1:T(1,128)S(1)}, s32[64,1]{0,1:T(1,128)}, u32[]{:S(2)}) %copy-start.3) | copy-done | bytes 280
  2.9 0.0 copy-start.4
  2.9 3.4 %copy-done.4 = bf16[2048,2048]{1,0:T(8,128)(2,1)S(1)} copy-done((bf16[2048,2048]{1,0:T(8,128)(2,1)S(1)}, bf16[2048,2048]{1,0:T(8,128)(2,1)}, u32[]{:S(2)}) %copy-start.4) | copy-done | bytes 8388632
  6.3 0.0 copy-start.5
  6.3 1.2 %copy-done.5 = bf16[2048,256]{1,0:T(8,128)(2,1)S(1)} copy-done((bf16[2048,256]{1,0:T(8,128)(2,1)S(1)}, bf16[2048,256]{1,0:T(8,128)(2,1)}, u32[]{:S(2)}) %copy-start.5) | copy-done | bytes 1048600
  7.5 53.8 %shard_map.64 = bf16[12,16,32,256]{3,2,1,0:T(8,128)(2,1)S(1)} custom-call(bf16[64,2048]{1,0:T(8,128)(2,1)S(1)} %bitcast.4, s32[1,64]{1,0:T(1,128)S(1)} %bitcast.5, s32[1,64]{1,0:T(1,128)S(1)} %bitcast.6, s32[1,64]{1,0:T(1,128)S(1)} %bitcast.7, bf16[2048,2048]{1,0:T(8,128)(2,1)S(1)} %copy-done.4, bf16[2048,256]{1,0:T(8,128)(2,1)S(1)} %copy-done.5), custom_call_target="tpu_custom_call" | custom-call | flops 6442450944 | bytes 8388608 | tf_op jit(solution)/shard_map/pallas_call | solution.py:433
  61.3 1.7 %copy.8 = bf16[12,16,32,256]{3,2,1,0:T(8,128)(2,1)} copy(bf16[12,16,32,256]{3,2,1,0:T(8,128)(2,1)S(1)} %shard_map.64) | data formatting | bytes 6291456
Async XLA Ops:
  0.0 0.9 %copy-start = (bf16[1,64,2048]{2,1,0:T(8,128)(2,1)S(1)}, bf16[1,64,2048]{2,1,0:T(8,128)(2,1)}, u32[]{:S(2)}) copy-start(bf16[1,64,2048]{2,1,0:T(8,128)(2,1)} %param.6) | copy-start | bytes 786436
  1.0 0.7 %copy-start.1 = (s32[64]{0:T(128)S(1)}, s32[64]{0:T(128)}, u32[]{:S(2)}) copy-start(s32[64]{0:T(128)} %param.7) | copy-start | bytes 772
  1.6 0.7 %copy-start.2 = (s32[64]{0:T(128)S(1)}, s32[64]{0:T(128)}, u32[]{:S(2)}) copy-start(s32[64]{0:T(128)} %param.8) | copy-start | bytes 772
  2.3 0.7 %copy-start.3 = (s32[64,1]{0,1:T(1,128)S(1)}, s32[64,1]{0,1:T(1,128)}, u32[]{:S(2)}) copy-start(s32[64,1]{0,1:T(1,128)} %param.9) | copy-start | bytes 772
  2.9 3.4 %copy-start.4 = (bf16[2048,2048]{1,0:T(8,128)(2,1)S(1)}, bf16[2048,2048]{1,0:T(8,128)(2,1)}, u32[]{:S(2)}) copy-start(bf16[2048,2048]{1,0:T(8,128)(2,1)} %constant.4.clone.forward_hbm) | copy-start | bytes 25165828
  6.3 1.2 %copy-start.5 = (bf16[2048,256]{1,0:T(8,128)(2,1)S(1)}, bf16[2048,256]{1,0:T(8,128)(2,1)}, u32[]{:S(2)}) copy-start(bf16[2048,256]{1,0:T(8,128)(2,1)} %constant.5.clone.back_ref) | copy-start | bytes 3145732

commit v4 on v3

--- a/solution.py
+++ b/solution.py
@@ -143,9 +143,9 @@
 
 
 def fused_kernel(
-    chips, slots, traces_ref, live_ref, sources_ref, owners_ref, forward_hbm, back_ref, out_hbm,
-    forward, samples, given_in, picked, core_in, part, parts_in, chosen, white_source, everyone,
-    cross_even, cross_odd, finished, table_sem, out_sem, pair_send, pair_recv, deal_send, deal_recv, share_send, share_recv,
+    chips, slots, traces_hbm, live_hbm, sources_hbm, owners_hbm, forward_hbm, back_hbm, out_hbm,
+    traces_ref, live_ref, sources_ref, owners_ref, back_ref, in_sem, forward, samples, given_in, picked, core_in, part, parts_in, chosen, white_source, everyone,
+    cross_even, cross_odd, joined, own, finished, table_sem, out_sem, pair_send, pair_recv, deal_send, deal_recv, share_send, share_recv,
     right_send, right_recv, left_send, left_recv, twin_send, twin_recv,
 ):
     lines = chips // 2
@@ -172,6 +172,15 @@
             device_id=peer, device_id_type=pl.DeviceIdType.MESH,
         )
 
+    inputs = [
+        pltpu.make_async_copy(source, target, in_sem.at[index])
+        for index, (source, target) in enumerate((
+            (sources_hbm, sources_ref), (owners_hbm, owners_ref), (live_hbm, live_ref),
+            (traces_hbm, traces_ref), (back_hbm, back_ref),
+        ))
+    ]
+    for copy in inputs:
+        copy.start()
     table_copy = pltpu.make_async_copy(forward_hbm, forward, table_sem)
     table_copy.start()
     twin = {"row": chip * 2 + 1 - core}
@@ -180,6 +189,9 @@
     barrier = pltpu.get_barrier_semaphore()
     for peer in [twin, across] + peers:
         pl.semaphore_signal(barrier, inc=1, device_id=peer, device_id_type=pl.DeviceIdType.MESH)
+
+    for copy in inputs:
+        copy.wait()
 
     def ids(shape, axis):
         return lax.broadcasted_iota(jnp.int32, shape, axis).astype(jnp.float32)
@@ -234,32 +246,34 @@
     for copy in deals:
         copy.start()
 
-    def whiten(traces):
-        count = traces.shape[0]
-        real = jnp.dot(traces, forward[:, :NF], preferred_element_type=jnp.float32)
-        imag = jnp.dot(traces, forward[:, NF:], preferred_element_type=jnp.float32)
-        first = lax.broadcasted_iota(jnp.int32, (2 * BAND, 2 * BAND), 0) // BAND
-        second = lax.broadcasted_iota(jnp.int32, (2 * BAND, 2 * BAND), 1) // BAND
+    chunk = 4 * BAND
+
+    def whiten(traces, target):
+        first = lax.broadcasted_iota(jnp.int32, (chunk, chunk), 0) // BAND
+        second = lax.broadcasted_iota(jnp.int32, (chunk, chunk), 1) // BAND
         same = jnp.where(first == second, 1.0, 0.0).astype(jnp.bfloat16)
-        power = real * real + imag * imag
-        scales = []
-        for low in range(0, NF, 2 * BAND):
-            piece = power[:, low : low + 2 * BAND]
-            upper = piece.astype(jnp.bfloat16)
-            lower = (piece - upper.astype(jnp.float32)).astype(jnp.bfloat16)
+
+        @pl.loop(0, NF // chunk)
+        def _(step):
+            low = pl.ds(pl.multiple_of(step * chunk, chunk), chunk)
+            high = pl.ds(pl.multiple_of(NF + step * chunk, chunk), chunk)
+            real = jnp.dot(traces[...], forward[:, low], preferred_element_type=jnp.float32)
+            imag = jnp.dot(traces[...], forward[:, high], preferred_element_type=jnp.float32)
+            power = real * real + imag * imag
+            upper = power.astype(jnp.bfloat16)
+            lower = (power - upper.astype(jnp.float32)).astype(jnp.bfloat16)
             total = jnp.dot(upper, same, preferred_element_type=jnp.float32) + jnp.dot(
                 lower, same, preferred_element_type=jnp.float32
             )
-            scales.append(lax.rsqrt(total / (2 * BAND) + 1e-05))
-        scaling = jnp.concatenate(scales, axis=1)
-        return (real * scaling).astype(jnp.bfloat16), (imag * scaling).astype(jnp.bfloat16)
+            scaling = lax.rsqrt(total / (2 * BAND) + 1e-05)
+            target[:, low] = (real * scaling).astype(jnp.bfloat16)
+            target[:, high] = (imag * scaling).astype(jnp.bfloat16)
 
     table_copy.wait()
     swap.wait_recv()
-    kept = samples[rows_of(seg * receivers, receivers), :]
-    real, imag = whiten(jnp.concatenate([kept, given_in[...]], axis=0))
-    everyone[row, :, :NF] = real
-    everyone[row, :, NF:] = imag
+    joined[:receivers] = samples[rows_of(seg * receivers, receivers), :]
+    joined[receivers:] = given_in[...]
+    whiten(joined, everyone.at[row])
 
     def shard(where, stream, piece):
         return everyone.at[chip_at(where) * 2 + stream, pl.ds(piece * receivers, receivers)]
@@ -277,27 +291,19 @@
         block = shard(place + hop - 1, core, piece)
         return remote(block, block, left_send.at[index], left_recv.at[index], left_peer)
 
-    order = [0]
-    for hop in range(1, half):
-        order += [-hop, hop]
-    order.append(-half)
+    def offset_of(number):
+        return (number + 1) // 2 * (1 - 2 * (number % 2))
 
     def to_twin(number, piece):
         index = number * 2 + piece
-        block = shard(place + order[number], core, piece)
+        block = shard(place + offset_of(number), core, piece)
         return remote(block, block, twin_send.at[index], twin_recv.at[index], twin)
 
-    started = []
-
-    def go(copy):
-        copy.start()
-        started.append(copy)
-
     for piece in range(2):
-        go(right(1, piece))
-        go(left(1, piece))
+        right(1, piece).start()
+        left(1, piece).start()
     for piece in range(2):
-        go(to_twin(0, piece))
+        to_twin(0, piece).start()
 
     for copy in deals:
         copy.wait_recv()
@@ -324,16 +330,25 @@
     here.start()
 
     def event(hop, piece):
-        if hop < half or piece == 0:
+        @pl.when((hop < half) | (piece == 0))
+        def _():
             right(hop, piece).wait_recv()
-            if hop + 1 < half or (hop + 1 == half and piece == 0):
-                go(right(hop + 1, piece))
-            go(to_twin(2 * hop - 1, piece))
-        if hop < half or piece == 1:
+
+            @pl.when((hop + 1 < half) | ((hop + 1 == half) & (piece == 0)))
+            def _():
+                right(hop + 1, piece).start()
+
+            to_twin(2 * hop - 1, piece).start()
+
+        @pl.when((hop < half) | (piece == 1))
+        def _():
             left(hop, piece).wait_recv()
-            if hop + 1 < half or (hop + 1 == half and piece == 1):
-                go(left(hop + 1, piece))
-            go(to_twin(2 * hop if hop < half else 2 * hop - 1, piece))
+
+            @pl.when((hop + 1 < half) | ((hop + 1 == half) & (piece == 1)))
+            def _():
+                left(hop + 1, piece).start()
+
+            to_twin(2 * hop - hop // half, piece).start()
 
     event(1, 0)
     event(1, 1)
@@ -345,16 +360,11 @@
     here.wait_recv()
     event(2, 0)
     there.wait_recv()
-    own = jnp.concatenate(
-        [
-            jnp.dot(choose, chosen[which], preferred_element_type=jnp.float32).astype(jnp.bfloat16)
-            for which in range(2)
-        ],
-        axis=0,
-    )
-    real, imag = whiten(own)
-    white_source[:, :NF] = real
-    white_source[:, NF:] = imag
+    for which in range(2):
+        own[which * padded : (which + 1) * padded] = jnp.dot(
+            choose, chosen[which], preferred_element_type=jnp.float32
+        ).astype(own.dtype)
+    whiten(own, white_source)
 
     def cross_block(block, cross):
         for slot in range(slots):
@@ -379,43 +389,51 @@
         normed = (stacked * lax.rsqrt(mean_sq + 1e-06)).astype(finished.dtype)
         for slot in range(slots):
             finished[block, slot] = normed[slot * receivers : (slot + 1) * receivers]
-        copy = pltpu.make_async_copy(finished.at[block], out_hbm.at[:, block], out_sem.at[index])
-        copy.start()
-        written.append(copy)
-
-    written = []
-    waiting = []
-
-    def finish_waiting():
-        while waiting:
-            finish_block(*waiting.pop())
-
-    def correlate_chip(number):
+        write(block, index).start()
+
+    def write(block, index):
+        return pltpu.make_async_copy(finished.at[block], out_hbm.at[:, block], out_sem.at[index])
+
+    def block_of(number, stream):
+        return chip_at(place + offset_of(number)) * 2 + stream
+
+    ahead = 3
+
+    @pl.loop(0, chips)
+    def _(number):
+        now = number + ahead
+
+        @pl.when(now < 2 * half)
+        def _():
+            event(now // 2 + 1, now % 2)
+
         for piece in range(2):
             to_twin(number, piece).wait_recv()
-        where = chip_at(place + order[number])
-        for stream, cross in enumerate((cross_even, cross_odd)):
-            block = where * 2 + stream
-            finish_waiting()
-            cross_block(block, cross)
-            waiting.append((block, cross, number * 2 + stream))
-
-    event(2, 1)
-    correlate_chip(0)
-    number = 1
-    for hop in range(3, half + 1):
+        cross_block(block_of(number, 0), cross_even)
+        finish_block(block_of(number, 0), cross_even, number * 2)
+        cross_block(block_of(number, 1), cross_odd)
+        finish_block(block_of(number, 1), cross_odd, number * 2 + 1)
+
+    for copy in deals + shares + [swap, fold, over, here, there]:
+        copy.wait_send()
+
+    @pl.loop(0, 2 * half)
+    def _(now):
+        hop, piece = now // 2 + 1, now % 2
+
+        @pl.when((hop < half) | (piece == 0))
+        def _():
+            right(hop, piece).wait_send()
+
+        @pl.when((hop < half) | (piece == 1))
+        def _():
+            left(hop, piece).wait_send()
+
+    @pl.loop(0, chips)
+    def _(number):
         for piece in range(2):
-            event(hop, piece)
-            correlate_chip(number)
-            number += 1
-    while number < chips:
-        correlate_chip(number)
-        number += 1
-    finish_waiting()
-    for copy in deals + shares + started + [swap, fold, over, here, there]:
-        copy.wait_send()
-    for copy in written:
-        copy.wait()
+            to_twin(number, piece).wait_send()
+            write(block_of(number, piece), number * 2 + piece).wait()
 
 
 def paired(forward, back, traces, live_mask, sources, owners):
@@ -427,15 +445,21 @@
     slots = 3 * num_sources // row_count
     padded = -(-slots // 16) * 16
     kind = traces.dtype
-    whole = pl.BlockSpec(memory_space=pltpu.VMEM)
+    anywhere = pl.BlockSpec(memory_space=pl.ANY)
     dma = pltpu.SemaphoreType.DMA
     hops = chips // 2 * 2
     return pl.pallas_call(
         partial(fused_kernel, chips, slots),
-        in_specs=[whole] * 4 + [pl.BlockSpec(memory_space=pltpu.HBM), whole],
-        out_specs=pl.BlockSpec(memory_space=pl.ANY),
+        in_specs=[anywhere] * 6,
+        out_specs=anywhere,
         out_shape=jax.ShapeDtypeStruct((slots, row_count, receivers, LAGS), jnp.bfloat16),
         scratch_shapes=[
+            pltpu.VMEM((channels, width), kind),
+            pltpu.VMEM((1, channels), jnp.int32),
+            pltpu.VMEM((1, num_sources), jnp.int32),
+            pltpu.VMEM((1, num_sources), jnp.int32),
+            pltpu.VMEM(back.shape, kind),
+            dma((5,)),
             pltpu.VMEM(forward.shape, kind),
             pltpu.VMEM((channels, width), kind),
             pltpu.VMEM((receivers, width), kind),
@@ -448,6 +472,8 @@
             pltpu.VMEM((row_count, channels, 2 * NF), kind),
             pltpu.VMEM((slots * receivers, 2 * NF), kind),
             pltpu.VMEM((slots * receivers, 2 * NF), kind),
+            pltpu.VMEM((channels, width), kind),
+            pltpu.VMEM((2 * padded, width), kind),
             pltpu.VMEM((row_count, slots, receivers, LAGS), kind),
             dma,
             dma((row_count,)),
@@ -459,7 +485,7 @@
             dma((2 * chips,)), dma((2 * chips,)),
         ],
         compiler_params=pltpu.CompilerParams(
-            collective_id=0, has_side_effects=True, vmem_limit_bytes=30 << 20
+            collective_id=0, has_side_effects=True, vmem_limit_bytes=56 << 20
         ),
         cost_estimate=pl.CostEstimate(
             flops=2 * slots * row_count * receivers * 2 * NF * LAGS,

time: 63.3 us -> 50.9 us (0.80)
  Pallas kernels: 53.8 us -> 46.8 us
  local copies, waits for them, and re-layouts: 9.19 us -> 3.86 us
    pallas_call x1, Pallas kernels: 53.8 us -> 46.8 us  [paired(): pl.pallas_call(partial(fused_kernel, chips, slots), in_specs=[anywhere] *...]
    unnamed x13 -> x1, local copies, waits for them, and re-layouts: 9.19 us -> 3.86 us
where the time goes in v4:
time: 50.9 us; the launch traced here: 50.7 us
  Pallas kernels  46.8 us (92%)
  local copies, waits for them, and re-layouts  3.86 us (8%)
    pallas_call x1, Pallas kernels, paired(): pl.pallas_call(partial(fused_kernel, chips, slots), in_specs=[anywhere] *...  46.8 us
    unnamed x1, local copies, waits for them, and re-layouts  3.86 us

profile of v4, /device:TPU:0, one launch (start us, length us, event | category | flops | bytes accessed | tf_op | source)
XLA Modules:
  0.0 50.7 jit_solution(2999264335878905366)
XLA Ops:
  0.0 46.8 %shard_map.64 = bf16[12,16,32,256]{3,2,1,0:T(8,128)(2,1)} custom-call(bf16[64,2048]{1,0:T(8,128)(2,1)} %bitcast.4, s32[1,64]{1,0:T(1,128)} %bitcast.5, s32[1,64]{1,0:T(1,128)} %bitcast.6, s32[1,64]{1,0:T(1,128)} %bitcast.7, bf16[2048,2048]{1,0:T(8,128)(2,1)} %constant.4.clone.forward_hbm, bf16[2048,256]{1,0:T(8,128)(2,1)} %constant.5.clone.back_hbm), custom_call_target="tpu_custom_call" | custom-call | flops 6442450944 | bytes 8388608 | tf_op jit(solution)/shard_map/pallas_call | solution.py:451
  46.8 3.9 %copy.8 = bf16[12,16,32,256]{3,2,1,0:T(8,128)(2,1)} copy(bf16[12,16,32,256]{3,2,1,0:T(8,128)(2,1)} %shard_map.64) | data formatting | bytes 6291456

commit v5 on v4

--- a/solution.py
+++ b/solution.py
@@ -269,42 +269,6 @@
             target[:, low] = (real * scaling).astype(jnp.bfloat16)
             target[:, high] = (imag * scaling).astype(jnp.bfloat16)
 
-    table_copy.wait()
-    swap.wait_recv()
-    joined[:receivers] = samples[rows_of(seg * receivers, receivers), :]
-    joined[receivers:] = given_in[...]
-    whiten(joined, everyone.at[row])
-
-    def shard(where, stream, piece):
-        return everyone.at[chip_at(where) * 2 + stream, pl.ds(piece * receivers, receivers)]
-
-    right_peer = {"row": chip_at(place + 1) * 2 + core}
-    left_peer = {"row": chip_at(place - 1) * 2 + core}
-
-    def right(hop, piece):
-        index = (hop - 1) * 2 + piece
-        block = shard(place - hop + 1, core, piece)
-        return remote(block, block, right_send.at[index], right_recv.at[index], right_peer)
-
-    def left(hop, piece):
-        index = (hop - 1) * 2 + piece
-        block = shard(place + hop - 1, core, piece)
-        return remote(block, block, left_send.at[index], left_recv.at[index], left_peer)
-
-    def offset_of(number):
-        return (number + 1) // 2 * (1 - 2 * (number % 2))
-
-    def to_twin(number, piece):
-        index = number * 2 + piece
-        block = shard(place + offset_of(number), core, piece)
-        return remote(block, block, twin_send.at[index], twin_recv.at[index], twin)
-
-    for piece in range(2):
-        right(1, piece).start()
-        left(1, piece).start()
-    for piece in range(2):
-        to_twin(0, piece).start()
-
     for copy in deals:
         copy.wait_recv()
     total = part[:, columns_of(chip)].astype(jnp.float32)
@@ -318,6 +282,42 @@
     ]
     for copy in shares:
         copy.start()
+    table_copy.wait()
+    swap.wait_recv()
+    joined[:receivers] = samples[rows_of(seg * receivers, receivers), :]
+    joined[receivers:] = given_in[...]
+    whiten(joined, everyone.at[row])
+
+    def shard(where, stream, piece):
+        return everyone.at[chip_at(where) * 2 + stream, pl.ds(piece * receivers, receivers)]
+
+    right_peer = {"row": chip_at(place + 1) * 2 + core}
+    left_peer = {"row": chip_at(place - 1) * 2 + core}
+
+    def right(hop, piece):
+        index = (hop - 1) * 2 + piece
+        block = shard(place - hop + 1, core, piece)
+        return remote(block, block, right_send.at[index], right_recv.at[index], right_peer)
+
+    def left(hop, piece):
+        index = (hop - 1) * 2 + piece
+        block = shard(place + hop - 1, core, piece)
+        return remote(block, block, left_send.at[index], left_recv.at[index], left_peer)
+
+    def offset_of(number):
+        return (number + 1) // 2 * (1 - 2 * (number % 2))
+
+    def to_twin(number, piece):
+        index = number * 2 + piece
+        block = shard(place + offset_of(number), core, piece)
+        return remote(block, block, twin_send.at[index], twin_recv.at[index], twin)
+
+    for piece in range(2):
+        right(1, piece).start()
+        left(1, piece).start()
+    for piece in range(2):
+        to_twin(0, piece).start()
+
     for copy in shares:
         copy.wait_recv()
     over = remote(

time: 50.9 us -> 48.7 us (0.957)
  Pallas kernels: 46.8 us -> 44.7 us
    pallas_call x1, Pallas kernels: 46.8 us -> 44.7 us  [paired(): pl.pallas_call(partial(fused_kernel, chips, slots), in_specs=[anywhere] *...]
where the time goes in v5:
time: 48.7 us; the launch traced here: 48.6 us
  Pallas kernels  44.7 us (92%)
  local copies, waits for them, and re-layouts  3.86 us (8%)
    pallas_call x1, Pallas kernels, paired(): pl.pallas_call(partial(fused_kernel, chips, slots), in_specs=[anywhere] *...  44.7 us
    unnamed x1, local copies, waits for them, and re-layouts  3.86 us

profile of v5, /device:TPU:0, one launch (start us, length us, event | category | flops | bytes accessed | tf_op | source)
XLA Modules:
  0.0 48.6 jit_solution(12772110128659122851)
XLA Ops:
  0.0 44.7 %shard_map.64 = bf16[12,16,32,256]{3,2,1,0:T(8,128)(2,1)} custom-call(bf16[64,2048]{1,0:T(8,128)(2,1)} %bitcast.4, s32[1,64]{1,0:T(1,128)} %bitcast.5, s32[1,64]{1,0:T(1,128)} %bitcast.6, s32[1,64]{1,0:T(1,128)} %bitcast.7, bf16[2048,2048]{1,0:T(8,128)(2,1)} %constant.4.clone.forward_hbm, bf16[2048,256]{1,0:T(8,128)(2,1)} %constant.5.clone.back_hbm), custom_call_target="tpu_custom_call" | custom-call | flops 6442450944 | bytes 8388608 | tf_op jit(solution)/shard_map/pallas_call | solution.py:451
  44.7 3.9 %copy.8 = bf16[12,16,32,256]{3,2,1,0:T(8,128)(2,1)} copy(bf16[12,16,32,256]{3,2,1,0:T(8,128)(2,1)} %shard_map.64) | data formatting | bytes 6291456
